TPU v7x, 128 devices: a whole 4x4x4 slice. The times are simulated.
128 devices in a mesh: seq: 128 (over x, y, z, core).
Axes of the slice: x: 4, y: 4, z: 4, core: 2. Of those that a mesh axis runs over, the one named last changes fastest.
Arguments:
- parent_rows: bfloat16 [32768, 512], P('seq'), may hold values from -50 to 50, as said below
- counts: int32 [32768], P('seq'), may hold values from 0 to 8, as said below
- occupancy: int32 [65536], P('seq'), may hold values from 1 to 255
- sib_table: bfloat16 [8, 512], replicated, may hold values from -6 to 6
- gain: float32 [512], replicated, may hold values from 0.1 to 1.9
- w_qkv: bfloat16 [512, 1536], replicated, may hold values from -0.25 to 0.25
- w_out: bfloat16 [512, 512], replicated, may hold values from -0.25 to 0.25
- w_head: bfloat16 [512, 8], replicated, may hold values from -0.25 to 0.25
Outputs:
- grad_qkv: float32 [512, 1536], replicated
- grad_out: float32 [512, 512], replicated
- grad_head: float32 [512, 8], replicated
- grad_gain: float32 [512], replicated
- grad_sib: float32 [8, 512], replicated
Inputs may be any that keep to these rules, and one draw needn't show every extreme that they name: `parent_rows`: each value is a random draw times a scale of its row and a scale of its column. The counts add up to 65536. The children of the parents held by device k form the contiguous range of nodes given by the counts, and lie on devices k-1, k and k+1. In each device's 256 parents, some parent has 8 children and some has none.
All inputs are finite; a program needn't handle non-finite values.
Results may differ from a plain program's by a relative error of at most 0.0045.
Values may be sent and summed in bfloat16 or wider, within the bound.
A program may use at most 128 MiB of HBM per device.

v0:
```python
import jax
import jax.numpy as jnp
from jax import lax
from jax.sharding import Mesh
from jax.sharding import PartitionSpec as P

HEADS = 4
SEQ = ("seq_0", "seq_1", "seq_2", "seq_3")


highest = lax.Precision.HIGHEST


def neutral_like(value, identity):
    return jnp.broadcast_to(jnp.asarray(identity, value.dtype), value.shape)


def entering(value, axes, combine, identity):
    before = start = neutral_like(value, identity)
    subtotal = value
    for axis in reversed(axes):
        length, place = (lax.axis_size(axis), lax.axis_index(axis))
        pieces = lax.all_gather(subtotal, axis)
        inside, subtotal = (start, start)
        for k in range(length):
            passed = k < place
            subtotal = combine(subtotal, pieces[k])
            inside = jnp.where(passed, subtotal, inside)
        before = combine(inside, before)
    return before


def padded(block, sides, width):
    for axis, dim in sides:
        count = lax.axis_size(axis)
        forward = [(i, i + 1) for i in range(count - 1)]
        backward = [(target, source) for source, target in forward]
        low = lax.ppermute(
            lax.slice_in_dim(block, block.shape[dim] - width, None, axis=dim), axis, forward
        )
        high = lax.ppermute(lax.slice_in_dim(block, 0, width, axis=dim), axis, backward)
        block = jnp.concatenate([low, block, high], axis=dim)
    return block


def entering_2(value, axes, combine, identity):
    before = start = neutral_like(value, identity)
    subtotal = value
    for axis in reversed(axes):
        length, place = (lax.axis_size(axis), lax.axis_index(axis))
        pieces = lax.all_gather(subtotal.astype(jnp.bfloat16), axis)
        inside, subtotal = (start, start)
        for k in reversed(range(length)):
            passed = k > place
            subtotal = combine(subtotal, pieces[k].astype(value.dtype))
            inside = jnp.where(passed, subtotal, inside)
        before = combine(inside, before)
    return before


def add_terms(earlier, later):
    return earlier + later


def head_slice(packed, part, head_id, width):
    head_size = width // HEADS
    begin = part * width + head_id * head_size
    return packed[:, begin : begin + head_size]


def normalize_inputs(inputs, gain):
    inputs_f = inputs.astype(jnp.float32)
    inv_in = lax.rsqrt(jnp.mean(inputs_f * inputs_f, axis=-1, keepdims=True) + 1e-06)
    normed = (inputs_f * inv_in * gain).astype(jnp.bfloat16)
    return (inputs_f, inv_in, normed)


def local_states(packed, width):
    return jnp.stack(
        [
            jnp.dot(
                head_slice(packed, 1, head_id, width).T,
                head_slice(packed, 2, head_id, width),
                preferred_element_type=jnp.float32,
            )
            for head_id in range(HEADS)
        ]
    )


def query_states(packed, grads, width):
    return jnp.stack(
        [
            jnp.dot(
                head_slice(packed, 0, head_id, width).T,
                grads[head_id],
                preferred_element_type=jnp.float32,
            )
            for head_id in range(HEADS)
        ]
    )


def causal_mask(count):
    return jnp.tril(jnp.ones((count, count), jnp.bool_))


def attend(packed, prefix, width):
    causal = causal_mask(packed.shape[0])
    scores = []
    numers = []
    inverses = []
    pieces = []
    for head_id in range(HEADS):
        queries = head_slice(packed, 0, head_id, width)
        keys_here = head_slice(packed, 1, head_id, width)
        values_here = head_slice(packed, 2, head_id, width)
        score = jnp.where(
            causal, jnp.dot(queries, keys_here.T, preferred_element_type=jnp.float32), 0.0
        )
        numer = jnp.dot(score, values_here.astype(jnp.float32), precision=highest) + jnp.dot(
            queries.astype(jnp.float32), prefix[head_id], precision=highest
        )
        inverse = lax.rsqrt(jnp.mean(numer * numer, axis=-1, keepdims=True) + 1e-05)
        scores.append(score)
        numers.append(numer)
        inverses.append(inverse)
        pieces.append(numer * inverse)
    attended = jnp.concatenate(pieces, axis=1).astype(jnp.bfloat16)
    return (scores, numers, inverses, attended)


def readout(inputs_f, attended, w_out, w_head):
    resid = inputs_f + jnp.dot(attended, w_out, preferred_element_type=jnp.float32)
    inv_out = lax.rsqrt(jnp.mean(resid * resid, axis=-1, keepdims=True) + 1e-06)
    final = (resid * inv_out).astype(jnp.bfloat16)
    logits = jnp.dot(final, w_head, preferred_element_type=jnp.float32)
    return (resid, inv_out, final, logits)


def output_grads(occupancy, logits, final, resid, inv_out, w_head, scale):
    powers = 2 ** jnp.arange(w_head.shape[1], dtype=jnp.int32)
    target = (occupancy[:, None] // powers[None, :] % 2).astype(jnp.float32)
    d_logits = ((jax.nn.sigmoid(logits) - target) * scale).astype(jnp.bfloat16)
    grad_head = jnp.dot(final.T, d_logits, preferred_element_type=jnp.float32)
    d_final = jnp.dot(d_logits, w_head.T, preferred_element_type=jnp.float32)
    d_resid = inv_out * d_final - resid * inv_out**3 * jnp.mean(
        d_final * resid, axis=-1, keepdims=True
    )
    return (grad_head, d_resid)


def numer_grads(attended, d_resid, numers, inverses, w_out, width):
    d_resid_b = d_resid.astype(jnp.bfloat16)
    grad_out = jnp.dot(attended.T, d_resid_b, preferred_element_type=jnp.float32)
    d_attended = jnp.dot(d_resid_b, w_out.T, preferred_element_type=jnp.float32)
    head_size = width // HEADS
    grads = []
    for head_id in range(HEADS):
        piece = d_attended[:, head_id * head_size : (head_id + 1) * head_size]
        numer = numers[head_id]
        inverse = inverses[head_id]
        d_numer = inverse * piece - numer * inverse**3 * jnp.mean(
            piece * numer, axis=-1, keepdims=True
        )
        grads.append(d_numer.astype(jnp.bfloat16))
    return (grad_out, grads)


def attention_grads(packed, scores, grads, prefix, suffix, width):
    causal = causal_mask(packed.shape[0])
    d_queries = []
    d_keys = []
    d_values = []
    for head_id in range(HEADS):
        queries = head_slice(packed, 0, head_id, width)
        keys_here = head_slice(packed, 1, head_id, width)
        values_here = head_slice(packed, 2, head_id, width)
        grad = grads[head_id]
        grad_f = grad.astype(jnp.float32)
        back = jnp.where(
            causal, jnp.dot(grad, values_here.T, preferred_element_type=jnp.float32), 0.0
        )
        d_queries.append(
            jnp.dot(back, keys_here.astype(jnp.float32), precision=highest)
            + jnp.dot(grad_f, prefix[head_id].T, precision=highest)
        )
        d_keys.append(
            jnp.dot(back.T, queries.astype(jnp.float32), precision=highest)
            + jnp.dot(values_here.astype(jnp.float32), suffix[head_id].T, precision=highest)
        )
        d_values.append(
            jnp.dot(scores[head_id].T, grad_f, precision=highest)
            + jnp.dot(keys_here.astype(jnp.float32), suffix[head_id], precision=highest)
        )
    return jnp.concatenate(d_queries + d_keys + d_values, axis=1).astype(jnp.bfloat16)


def input_grads(inputs_f, inv_in, normed, d_packed, d_resid, onehot, gain, w_qkv):
    grad_qkv = jnp.dot(normed.T, d_packed, preferred_element_type=jnp.float32)
    d_normed = jnp.dot(d_packed, w_qkv.T, preferred_element_type=jnp.float32)
    grad_gain = jnp.sum(d_normed * inputs_f * inv_in, axis=0)
    d_scaled = d_normed * gain
    d_inputs = (
        inv_in * d_scaled
        - inputs_f * inv_in**3 * jnp.mean(d_scaled * inputs_f, axis=-1, keepdims=True)
        + d_resid
    )
    grad_sib = jnp.dot(onehot.T, d_inputs, precision=highest)
    return (grad_qkv, grad_gain, grad_sib)


def shards(parent_rows, counts, occupancy, sib_table, gain, w_qkv, w_out, w_head):
    parents_here = counts.shape[0]
    nodes_here = occupancy.shape[0]
    width = parent_rows.shape[1]
    local_end = jnp.cumsum(counts)
    offset = entering(local_end[-1], SEQ, add_terms, jnp.int32(0))
    ends = local_end + offset
    bounds = jnp.stack([ends - counts, ends], axis=1)
    window_rows, window_bounds = (
        padded(parent_rows, ((SEQ, 0),), parents_here),
        padded(bounds, ((SEQ, 0),), parents_here),
    )
    node_ids = lax.axis_index(SEQ) * nodes_here + jnp.arange(nodes_here, dtype=jnp.int32)
    window_ends = window_bounds[:, 1]
    slot_ids = jnp.arange(3 * parents_here, dtype=jnp.int32)
    usable = (slot_ids < 2 * parents_here) | (window_ends > 0)
    finished = (window_ends[None, :] <= node_ids[:, None]) & usable[None, :]
    parent_slot = jnp.sum(finished.astype(jnp.int32), axis=1)
    parent_feat = jnp.take(window_rows, parent_slot, axis=0)
    rank = node_ids - jnp.take(window_bounds[:, 0], parent_slot, axis=0)
    onehot = (rank[:, None] == jnp.arange(sib_table.shape[0], dtype=jnp.int32)[None, :]).astype(
        jnp.float32
    )
    inputs = (
        parent_feat.astype(jnp.float32)
        + jnp.dot(onehot.astype(jnp.bfloat16), sib_table, preferred_element_type=jnp.float32)
    ).astype(jnp.bfloat16)
    inputs_f, inv_in, normed = normalize_inputs(inputs, gain)
    packed = jnp.dot(normed, w_qkv, preferred_element_type=jnp.float32).astype(jnp.bfloat16)
    states = local_states(packed, width)
    prefix = entering(states, SEQ, add_terms, jnp.zeros_like(states))
    scores, numers, inverses, attended = attend(packed, prefix, width)
    resid, inv_out, final, logits = readout(inputs_f, attended, w_out, w_head)
    scale = float(lax.axis_size(SEQ) * nodes_here) ** (-0.5)
    grad_head, d_resid = output_grads(occupancy, logits, final, resid, inv_out, w_head, scale)
    grad_out, grads = numer_grads(attended, d_resid, numers, inverses, w_out, width)
    qstates = query_states(packed, grads, width)
    suffix = entering_2(qstates, SEQ, add_terms, jnp.zeros_like(qstates))
    d_packed = attention_grads(packed, scores, grads, prefix, suffix, width)
    grad_qkv, grad_gain, grad_sib = input_grads(
        inputs_f, inv_in, normed, d_packed, d_resid, onehot, gain, w_qkv
    )
    grad_qkv, grad_out, grad_head, grad_gain, grad_sib = lax.psum(
        (grad_qkv, grad_out, grad_head, grad_gain, grad_sib), SEQ
    )
    return (grad_qkv, grad_out, grad_head, grad_gain, grad_sib)


def solution(mesh):
    torus = Mesh(mesh.devices.reshape(4, 4, 4, 2), ("seq_0", "seq_1", "seq_2", "seq_3"))
    placed = (P(SEQ, None), P(SEQ), P(SEQ), P(), P(), P(), P(), P())
    return jax.shard_map(
        shards, mesh=torus, in_specs=placed, out_specs=(P(), P(), P(), P(), P()), check_vma=False
    )
```

profile of v0, /device:TPU:1, one launch (start us, length us, event | category | flops | bytes accessed | tf_op | source)
XLA Modules:
  0.0 399.7 jit_solution(7655104058552766727)
XLA Ops:
  7.3 1.1 reduce-window.9
  8.7 1.2 dynamic-slice
  9.9 0.8 slice_dynamic-update-slice_fusion
  10.7 1.2 dynamic-slice.1
  12.0 2.9 all-reduce
  14.9 0.6 fusion.154
  16.7 0.8 dynamic-update-slice.1
  17.5 1.2 dynamic-slice.2
  18.7 7.8 %all-reduce.1 = s32[4]{0:T(128)S(1)} all-reduce(s32[4]{0:T(128)S(1)} %dynamic-update-slice.1), channel_id=1, replica_groups=mesh['seq_0'=4,'seq_1'=4,'seq_2'=4,'seq_3'=2] {'seq_2'}, use_global_device_ids=true, to_apply=%add.1 | all-reduce | flops 4 | bytes 32
  26.5 0.6 fusion.153
  29.8 0.7 dynamic-update-slice.2
  30.4 1.3 dynamic-slice.3
  31.7 7.0 %all-reduce.2 = s32[4]{0:T(128)S(1)} all-reduce(s32[4]{0:T(128)S(1)} %dynamic-update-slice.2), channel_id=1, replica_groups=mesh['seq_0'=4,'seq_1'=4,'seq_2'=4,'seq_3'=2] {'seq_1'}, use_global_device_ids=true, to_apply=%add.2 | all-reduce | flops 4 | bytes 32
  38.7 0.7 fusion.152
  41.9 0.7 dynamic-update-slice.3
  42.6 6.9 %all-reduce.3 = s32[4]{0:T(128)S(1)} all-reduce(s32[4]{0:T(128)S(1)} %dynamic-update-slice.3), channel_id=1, replica_groups=mesh['seq_0'=4,'seq_1'=4,'seq_2'=4,'seq_3'=2] {'seq_0'}, use_global_device_ids=true, to_apply=%add.3 | all-reduce | flops 4 | bytes 32
  49.5 0.7 fusion.151
  55.3 0.7 add_subtract_fusion
  56.0 8.3 %collective-permute-start.1 = (s32[256,2]{0,1:T(2,128)S(1)}, s32[256,2]{0,1:T(2,128)S(1)}, u32[]{:S(2)}, u32[]{:S(2)}) collective-permute-start(s32[256,2]{0,1:T(2,128)S(1)} %pad_add_fusion.1), channel_id=1, source_target_pairs={{1,0},{2,1},{3,2},{4,3},{5,4},{6,5},{7,6},{8,7},{9,8},{10,9},{11,1... | collective-permute-start | bytes 6152 | tf_op jit(solution)/shard_map/ppermute | solution.py:41
  64.3 2.6 collective-permute-start
  66.8 2.4 collective-permute-start.2
  69.3 1.9 collective-permute-start.3
  71.7 2.3 gather_fusion.1
  74.0 3.1 collective-permute-done.3
  77.2 2.0 gather_fusion
  79.9 1.1 convolution_convert_fusion
  82.0 2.2 all-gather
  84.2 0.8 copy-done.13
  85.0 0.7 slice_add_fusion.9
  85.8 26.2 %all-gather.10.cloned.1.call-done = f32[16,128,128]{2,1,0:T(8,128)} async-done(((f32[4,128,128]{2,1,0:T(8,128)}), f32[16,128,128]{2,1,0:T(8,128)}) %all-gather.10.cloned.1.call-update) | async-done | bytes 1048592 | tf_op jit(solution)/shard_map/all_gather | solution.py:23
  112.0 1.9 fusion.68
  114.1 1.3 convolution_select_fusion.4
  115.4 23.1 %all-gather.6.cloned.1.call-done = f32[4,4,128,128]{3,2,1,0:T(8,128)} async-done(((f32[1,4,128,128]{3,2,1,0:T(8,128)}), f32[4,4,128,128]{3,2,1,0:T(8,128)}) %all-gather.6.cloned.1.call-update) | async-done | bytes 1048592 | tf_op jit(solution)/shard_map/all_gather | solution.py:23
  138.5 2.0 slice_add_fusion.3
  141.7 1.3 copy-done.7
  143.0 1.4 fusion.99
  144.4 1.4 fusion.109
  145.9 1.4 fusion.119
  147.3 0.7 fusion.130
  148.0 16.9 %all-gather.8.cloned.1.call-done = f32[4,4,128,128]{3,2,1,0:T(8,128)} async-done(((f32[1,4,128,128]{3,2,1,0:T(8,128)}), f32[4,4,128,128]{3,2,1,0:T(8,128)}) %all-gather.8.cloned.1.call-update) | async-done | bytes 1048592 | tf_op jit(solution)/shard_map/all_gather | solution.py:23
  164.9 2.4 fusion.67
  170.9 1.5 fusion.81
  173.3 0.7 copy-done.8
  177.7 0.5 fusion.82
  178.2 0.7 fusion.103
  179.3 0.5 fusion.87
  179.8 0.7 fusion.113
  180.8 0.7 fusion.92
  181.6 0.7 fusion.123
  182.6 0.5 fusion.138
  183.2 0.7 fusion.133
  183.9 3.2 all_gather.67
  187.2 11.4 %all_gather.68 = bf16[4,4,128,128]{3,2,1,0:T(8,128)(2,1)S(1)} all-gather(bf16[1,4,128,128]{3,2,1,0:T(8,128)(2,1)S(1)} %fusion.72), channel_id=1, replica_groups=mesh['seq_0'=4,'seq_1'=4,'seq_2'=4,'seq_3'=2] {'seq_2'}, dimensions={0}, use_global_device_ids=true | all-gather | bytes 655360 | tf_op jit(solution)/shard_map/all_gather | solution.py:51
  198.6 10.3 %all_gather.69 = bf16[4,4,128,128]{3,2,1,0:T(8,128)(2,1)S(1)} all-gather(bf16[1,4,128,128]{3,2,1,0:T(8,128)(2,1)S(1)} %fusion.71), channel_id=1, replica_groups=mesh['seq_0'=4,'seq_1'=4,'seq_2'=4,'seq_3'=2] {'seq_1'}, dimensions={0}, use_global_device_ids=true | all-gather | bytes 655360 | tf_op jit(solution)/shard_map/all_gather | solution.py:51
  209.0 10.2 %all_gather.70 = bf16[4,4,128,128]{3,2,1,0:T(8,128)(2,1)S(1)} all-gather(bf16[1,4,128,128]{3,2,1,0:T(8,128)(2,1)S(1)} %fusion.70), channel_id=1, replica_groups=mesh['seq_0'=4,'seq_1'=4,'seq_2'=4,'seq_3'=2] {'seq_0'}, dimensions={0}, use_global_device_ids=true | all-gather | bytes 655360 | tf_op jit(solution)/shard_map/all_gather | solution.py:51
  223.1 1.1 copy-done.17
  224.2 2.7 fusion.75
  227.0 1.0 copy-done.16
  228.0 2.7 fusion.45
  230.9 1.1 fusion.43
  232.0 72.6 %all-reduce.4 = (f32[512,8]{0,1:T(8,128)}, f32[512]{0:T(512)}, f32[8,512]{1,0:T(8,128)}) all-reduce(f32[512,8]{0,1:T(8,128)S(1)} %fusion.74, f32[512]{0:T(512)S(1)} %get-tuple-element.6, f32[8,512]{1,0:T(8,128)S(1)} %fusion.43), channel_id=1, replica_groups=mesh['seq_0'=4,'seq_1'=4,'seq_2'=4,'seq_3'=2] {'seq_0','seq_1','seq_2','..., use_global_device_ids=true, to_apply=%region_16.17 | all-reduce | flops 8704 | bytes 69632 | tf_op jit(solution)/shard_map/psum | solution.py:255
  304.6 83.8 %all-reduce.8.cloned.1.call-done = (f32[512,1536]{1,0:T(8,128)}, f32[512,512]{1,0:T(8,128)}) async-done(((f32[512,1536]{1,0:T(8,128)}, f32[512,512]{1,0:T(8,128)}), (f32[512,1536]{1,0:T(8,128)}, f32[512,512]{1,0:T(8,128)})) %all-reduce.8.cloned.1.call-update) | async-done | bytes 4194320 | tf_op jit(solution)/shard_map/psum | solution.py:255
  388.4 3.8 copy.57
  392.2 1.0 copy.58
  (149 shorter events, 17.1 us)
Async XLA Ops:
  7.2 72.8 %copy-start = (bf16[512,1536]{1,0:T(8,128)(2,1)S(1)}, bf16[512,1536]{1,0:T(8,128)(2,1)}, u32[]{:S(2)}) copy-start(bf16[512,1536]{1,0:T(8,128)(2,1)} %param.13) | copy-start | bytes 4718596
  7.2 70.0 %copy-start.23 = (bf16[256,512]{1,0:T(8,128)(2,1)S(1)}, bf16[256,512]{1,0:T(8,128)(2,1)}, u32[]{:S(2)}) copy-start(bf16[256,512]{1,0:T(8,128)(2,1)} %param.8) | copy-start | bytes 786436
  7.2 104.8 %all-gather.10.cloned.1.call-start = ((), (), s32[]{:S(2)}) async-start(), calls=%async_computation.2 | async-start | bytes 1310720 | tf_op jit(solution)/shard_map/all_gather | solution.py:23
  56.0 15.3 %collective-permute-start.1 = (s32[256,2]{0,1:T(2,128)S(1)}, s32[256,2]{0,1:T(2,128)S(1)}, u32[]{:S(2)}, u32[]{:S(2)}) collective-permute-start(s32[256,2]{0,1:T(2,128)S(1)} %pad_add_fusion.1), channel_id=1, source_target_pairs={{1,0},{2,1},{3,2},{4,3},{5,4},{6,5},{7,6},{8,7},{9,8},{10,9},{11,1... | collective-permute-start | bytes 6152 | tf_op jit(solution)/shard_map/ppermute | solution.py:41
  64.3 7.0 %collective-permute-start = (s32[256,2]{0,1:T(2,128)S(1)}, s32[256,2]{0,1:T(2,128)S(1)}, u32[]{:S(2)}, u32[]{:S(2)}) collective-permute-start(s32[256,2]{0,1:T(2,128)S(1)} %pad_add_fusion.1), channel_id=1, source_target_pairs={{0,1},{1,2},{2,3},{3,4},{4,5},{5,6},{6,7},{7,8},{8,9},{9,10},{10,1... | collective-permute-start | bytes 6152 | tf_op jit(solution)/shard_map/ppermute | solution.py:38
  66.8 7.2 %collective-permute-start.2 = (bf16[256,512]{1,0:T(8,128)(2,1)}, bf16[256,512]{1,0:T(8,128)(2,1)S(1)}, u32[]{:S(2)}, u32[]{:S(2)}) collective-permute-start(bf16[256,512]{1,0:T(8,128)(2,1)} %param.8), channel_id=1, source_target_pairs={{0,1},{1,2},{2,3},{3,4},{4,5},{5,6},{6,7},{7,8},{8,9},{9,10},{10,1... | collective-permute-start | bytes 786440 | tf_op jit(solution)/shard_map/ppermute | solution.py:38
  69.3 7.9 %collective-permute-start.3 = (bf16[256,512]{1,0:T(8,128)(2,1)}, bf16[256,512]{1,0:T(8,128)(2,1)S(1)}, u32[]{:S(2)}, u32[]{:S(2)}) collective-permute-start(bf16[256,512]{1,0:T(8,128)(2,1)} %param.8), channel_id=1, source_target_pairs={{1,0},{2,1},{3,2},{4,3},{5,4},{6,5},{7,6},{8,7},{9,8},{10,9},{11,1... | collective-permute-start | bytes 786440 | tf_op jit(solution)/shard_map/ppermute | solution.py:41
  77.2 2.2 copy-start.27
  79.2 0.7 copy-start.25
  79.9 1.1 copy-start.14
  81.1 87.5 %copy-start.1 = (bf16[512,1536]{1,0:T(8,128)(2,1)}, bf16[512,1536]{1,0:T(8,128)(2,1)S(1)}, u32[]{:S(2)}) copy-start(bf16[512,1536]{1,0:T(8,128)(2,1)S(1)} %convolution_convert_fusion) | copy-start | bytes 4718596
  82.0 32.0 %copy-start.26 = (s32[512]{0:T(512)S(1)}, s32[512]{0:T(512)}, u32[]{:S(2)}) copy-start(s32[512]{0:T(512)} %param.10) | copy-start | bytes 6148
  84.2 0.8 copy-start.13
  85.8 52.7 %all-gather.6.cloned.1.call-start = ((), (), s32[]{:S(2)}) async-start(), calls=%async_computation | async-start | bytes 1310720 | tf_op jit(solution)/shard_map/all_gather | solution.py:23
  114.0 50.9 %all-gather.8.cloned.1.call-start = ((), (), s32[]{:S(2)}) async-start(), calls=%async_computation.1 | async-start | bytes 1310720 | tf_op jit(solution)/shard_map/all_gather | solution.py:23
  140.5 247.9 %all-reduce.8.cloned.1.call-start = ((), (), s32[]{:S(2)}) async-start(), calls=%async_computation.3 | async-start | bytes 8388608 | tf_op jit(solution)/shard_map/psum | solution.py:255
  141.0 3.4 copy-start.11
  141.0 2.0 copy-start.7
  141.3 4.5 %copy-start.9 = (f32[512,512]{1,0:T(8,128)}, f32[512,512]{1,0:T(8,128)S(1)}, u32[]{:S(2)}) copy-start(f32[512,512]{1,0:T(8,128)S(1)} %convolution_select_fusion.6) | copy-start | bytes 3145732
  143.0 4.3 %copy-start.5 = (f32[512,512]{1,0:T(8,128)}, f32[512,512]{1,0:T(8,128)S(1)}, u32[]{:S(2)}) copy-start(f32[512,512]{1,0:T(8,128)S(1)} %convolution_select_fusion.7) | copy-start | bytes 3145732
  164.9 2.4 copy-start.21
  164.9 2.8 copy-start.20
  167.3 1.0 copy-start.19
  168.0 1.1 copy-start.15
  168.0 1.2 copy-start.22
  169.2 0.7 copy-start.24
  170.5 1.8 copy-start.3
  172.8 1.2 copy-start.8
  173.1 1.5 copy-start.2
  173.1 1.8 copy-start.12
  174.0 1.6 copy-start.10
  175.4 1.2 copy-start.6
  223.1 1.1 copy-start.17
  226.9 1.0 copy-start.16
  228.0 2.9 copy-start.4
  388.4 3.8 copy-start.18
Sparse Core Ops, SparseCore 0:
  85.9 26.0 all-gather.9
  114.1 24.3 all-gather.5
  140.6 24.2 all-gather.7
  227.1 161.2 all-reduce.7
where the time goes:
time: 401 us; the launch traced here: 400 us
  waiting for transfers between devices  153 us (38%)
  blocking collectives  134 us (33%)
  matrix products  33.5 us (8%)
  between operations  26.2 us (7%)
  local copies, waits for them, and re-layouts  25.8 us (6%)
  starting transfers between devices  15.5 us (4%)
  other arithmetic  11.1 us (3%)
    psum x1, waiting for transfers between devices, shards(): lax.psum((grad_qkv, grad_out, grad_head, grad_gain, grad_sib), SEQ)  83.8 us
    psum x1, blocking collectives, shards(): lax.psum((grad_qkv, grad_out, grad_head, grad_gain, grad_sib), SEQ)  72.6 us
    all_gather x3, waiting for transfers between devices, entering(): pieces = lax.all_gather(subtotal, axis)  66.2 us
    all_gather x4, blocking collectives, entering_2(): pieces = lax.all_gather(subtotal.astype(jnp.bfloat16), axis)  35.1 us
    unnamed x4, blocking collectives  24.6 us
    unnamed x70, local copies, waits for them, and re-layouts  18.7 us
    ppermute x2, starting transfers between devices, padded(): lax.ppermute(lax.slice_in_dim(block, 0, width, axis=dim), axis, backward)  10.2 us
  transfers between devices with their start and end apart: 8, of which 5 were waited for; matrix products, arithmetic and copies ran while one was open for 3% of the time, Pallas kernels for 0%

commit v1 on v0

v1 whole, which is shorter than its diff:
```python
import jax
import jax.numpy as jnp
from jax import lax
from jax.experimental import pallas as pl
from jax.experimental.pallas import tpu as pltpu
from jax.sharding import PartitionSpec as P

MESH = pl.DeviceIdType.MESH
F32, BF16 = jnp.float32, jnp.bfloat16
HEADS, HS, D = 4, 128, 512
N, PAR, DEVS = 512, 256, 128
RB = 128
BLOCKS = N // RB
COPIES = 160
PLANE = [(dx, dy) for dx in range(4) for dy in range(4) if dx or dy]


def dot(a, b):
    return jnp.dot(a, b, preferred_element_type=F32)


def dot_tn(a, b):
    return lax.dot_general(a, b, (((0,), (0,)), ((), ())), preferred_element_type=F32)


def dot_nt(a, b):
    return lax.dot_general(a, b, (((1,), (1,)), ((), ())), preferred_element_type=F32)


def split(value):
    high = value.astype(BF16)
    return high, (value - high.astype(F32)).astype(BF16)


def rows(start, count):
    return pl.ds(pl.multiple_of(start, count), count)


class Place:
    def __init__(self):
        me = lax.axis_index("seq")
        self.me = me
        self.x, self.y, self.z, self.c = me // 32, (me // 8) % 4, (me // 2) % 4, me % 2
        self.g = self.x * 4 + self.y
        self.sibling = me + 1 - 2 * self.c
        self.next = (me + 1) % DEVS
        self.prev = (me + DEVS - 1) % DEVS

    def line(self):
        for d in (1, 2, 3):
            zt = (self.z + d) % 4
            yield zt, self.me - 2 * self.z + 2 * zt

    def plane(self):
        for dx, dy in PLANE:
            xt, yt = (self.x + dx) % 4, (self.y + dy) % 4
            yield xt, yt, (xt * 4 + yt) * 8 + self.me % 8


class Links:
    def __init__(self, send, recv):
        self.send, self.recv, self.sent = send, recv, []

    def start(self, src, dst, device):
        k = len(self.sent)
        copy = pltpu.make_async_remote_copy(
            src_ref=src,
            dst_ref=dst,
            send_sem=self.send.at[k],
            recv_sem=self.recv.at[k],
            device_id=(device,),
            device_id_type=MESH,
        )
        copy.start()
        self.sent.append(copy)
        return copy

    def finish(self):
        for copy in self.sent:
            copy.wait_send()


def arrived(copies):
    for copy in copies:
        copy.wait_recv()


def greet(at):
    barrier = pltpu.get_barrier_semaphore()
    far = at.me + DEVS - 1 + 2 * at.c
    partners = [at.sibling, far % DEVS]
    partners += [dev for zt, dev in at.line()] + [dev for xt, yt, dev in at.plane()]
    for dev in partners:
        pl.semaphore_signal(barrier, inc=1, device_id=(dev,), device_id_type=MESH)
    pl.semaphore_wait(barrier, len(partners))


def scan(at, links, state, out, sib, chip, zbuf, pbuf, ret, ebuf, give, reverse):
    mine, other = rows(at.c * 256, 256), rows((1 - at.c) * 256, 256)
    first = links.start(state.at[other], sib, at.sibling)
    yield
    arrived([first])
    chip[...] = state[mine, :] + sib[...]
    copies = []
    for zt, dev in at.line():
        copies.append(links.start(chip.at[rows(zt * 64, 64)], zbuf.at[at.z], dev))
    zbuf[at.z] = chip[rows(at.z * 64, 64), :]
    yield
    arrived(copies)
    pbuf[at.g] = zbuf[0] + zbuf[1] + zbuf[2] + zbuf[3]
    copies = []
    for xt, yt, dev in at.plane():
        copies.append(links.start(pbuf.at[at.g], pbuf.at[at.g], dev))
    yield
    arrived(copies)
    total = jnp.zeros((64, HS), F32)
    for k in range(16):
        passed = (k > at.g) if reverse else (k < at.g)
        total = total + jnp.where(passed, pbuf[k], 0.0)
    for k in range(3, -1, -1) if reverse else range(4):
        ret[k] = total
        total = total + zbuf[k]
    copies = []
    for zt, dev in at.line():
        copies.append(links.start(ret.at[zt], ebuf.at[at.z], dev))
    ebuf[at.z] = ret[at.z]
    yield
    arrived(copies)
    first_core = at.c == (1 if reverse else 0)
    before = ebuf[...].reshape(256, HS)
    give[...] = before + jnp.where(first_core, state[mine, :], 0.0)
    last = links.start(give, out.at[mine], at.sibling)
    out[mine, :] = before + jnp.where(first_core, 0.0, sib[...])
    yield
    arrived([last])


def reduce_all(at, links, src, out, r0, r1, zb, r2, pb, small=None):
    mine, other = rows(at.c * 256, 256), rows((1 - at.c) * 256, 256)
    copies = [links.start(src.at[other], r0, at.sibling)]
    if small:
        xs, xo, x0, x1, xz = small
        xmine, xother = rows(at.c * 16, 16), rows((1 - at.c) * 16, 16)
        copies.append(links.start(xs.at[xother], x0, at.sibling))
    yield
    arrived(copies)
    for k in range(4):
        part = pl.ds(k * 64, 64)
        r1[part, :] = src[rows(at.c * 256 + k * 64, 64), :] + r0[part, :]
    copies = []
    if small:
        total = xs[xmine, :] + x0[...]
        for k in range(4):
            x1[k] = total[:, k * 128 : (k + 1) * 128]
        for zt, dev in at.line():
            copies.append(links.start(x1.at[zt], xz.at[at.z], dev))
        xz[at.z] = x1[at.z]
    for zt, dev in at.line():
        copies.append(links.start(r1.at[rows(zt * 64, 64)], zb.at[at.z], dev))
    yield
    arrived(copies)
    width = 384 if small else 256
    own = at.z * 64
    for k in range(16):
        xk, yk = k // 4, k % 4
        cols = pl.ds(yk * 256, 256)
        value = jnp.zeros((16, 256), F32)
        for j in range(4):
            piece = jnp.where(j == at.z, r1[rows(own + xk * 16, 16), cols], zb[j, pl.ds(xk * 16, 16), cols])
            value = value + piece
        r2[k, :, pl.ds(0, 256)] = value
    if small:
        value = xz[0] + xz[1] + xz[2] + xz[3]
        for k in range(16):
            r2[k, :, pl.ds(256, 128)] = value
    copies = []
    for xt, yt, dev in at.plane():
        copies.append(links.start(r2.at[xt * 4 + yt], pb.at[at.g], dev))
    pb[at.g] = r2[at.g]
    yield
    arrived(copies)
    total = pb[0]
    for k in range(1, 16):
        total = total + pb[k]
    place = out.at[rows(at.c * 256 + own + at.x * 16, 16), rows(at.y * 256, 256)]
    place[...] = total[:, :256]
    copies = []
    for xt, yt, dev in at.plane():
        copies.append(links.start(place, place, dev))
    if small:
        xplace = xo.at[xmine, rows(at.z * 128, 128)]
        xplace[...] = total[:, 256:]
        for zt, dev in at.line():
            copies.append(links.start(xplace, xplace, dev))
    yield
    arrived(copies)
    place = out.at[rows(at.c * 256 + own, 64)]
    copies = []
    for zt, dev in at.line():
        copies.append(links.start(place, place, dev))
    if small:
        copies.append(links.start(xo.at[xmine], xo.at[xmine], at.sibling))
    yield
    arrived(copies)
    last = links.start(out.at[mine], out.at[mine], at.sibling)
    yield
    arrived([last])


def step(generator):
    for _ in generator:
        return True
    return False


def finish(generator):
    while step(generator):
        pass


def head(h, part=0):
    return pl.ds(part * D + h * HS, HS)


def block(b):
    return pl.ds(b * RB, RB)


def lower(b):
    row = lax.broadcasted_iota(jnp.int32, (RB, (b + 1) * RB), 0) + b * RB
    col = lax.broadcasted_iota(jnp.int32, (RB, (b + 1) * RB), 1)
    return col <= row


def kernel(
    parents, counts, occupancy, sib_table, gain, w_qkv, w_out, w_head,
    early_out, late_out, small_out,
    window, ends, offz, offp, offs, inputs, inv_in, normed, packed, onehot,
    scores, numer, resid, inv_out, final, attended, d_logits, d_resid, d_resid_b, wide, grads, d_packed,
    d_local, states, prefix, qstates, suffix,
    f_sib, f_chip, f_z, f_p, f_ret, f_e, f_give,
    b_sib, b_chip, b_z, b_p, b_ret, b_e, b_give,
    early, e_r0, e_r1, e_z, e_r2, e_p,
    late, l_r0, l_r1, l_z, l_r2, l_p,
    small, x0, x1, xz,
    send, recv,
):
    at = Place()
    links = Links(send, recv)
    greet(at)

    own = pl.ds(PAR, PAR)
    tri = (
        lax.broadcasted_iota(jnp.int32, (PAR, PAR), 0) <= lax.broadcasted_iota(jnp.int32, (PAR, PAR), 1)
    ).astype(BF16)
    count = jnp.broadcast_to(counts[...].astype(F32), (16, PAR))
    local_ends = dot(count.astype(BF16), tri)[:8]
    whole = jnp.sum(count[:8], axis=1, keepdims=True)
    ends[1, :8] = local_ends
    ends[1, 8:] = count[:8]
    halo = [
        links.start(ends.at[1], ends.at[0], at.next),
        links.start(ends.at[1], ends.at[2], at.prev),
        links.start(parents, window.at[pl.ds(0, PAR)], at.next),
        links.start(parents, window.at[pl.ds(2 * PAR, PAR)], at.prev),
    ]
    window[own, :] = parents[...]

    offs[0] = jnp.broadcast_to(whole, (8, 128))
    first = links.start(offs.at[0], offs.at[1], at.sibling)
    arrived([first])
    offset = jnp.where(at.c == 1, offs[1], 0.0)
    offz[at.z] = offs[0] + offs[1]
    copies = [links.start(offz.at[at.z], offz.at[at.z], dev) for zt, dev in at.line()]
    arrived(copies)
    offp[at.g] = offz[0] + offz[1] + offz[2] + offz[3]
    copies = [links.start(offp.at[at.g], offp.at[at.g], dev) for xt, yt, dev in at.plane()]
    for k in range(4):
        offset = offset + jnp.where(k < at.z, offz[k], 0.0)
    arrived(copies)
    for k in range(16):
        offset = offset + jnp.where(k < at.g, offp[k], 0.0)
    shift = (at.me * N).astype(F32) - offset[:1, :1]

    arrived(halo)
    own_total = whole[:1, :1]
    low_total = ends[0, :1, PAR - 1 :]
    end_row = jnp.concatenate([ends[0, :1] - low_total, local_ends[:1], ends[2, :1] + own_total], axis=1)
    count_row = jnp.concatenate([ends[0, 8:9], count[:1], ends[2, 8:9]], axis=1)
    start_row = end_row - count_row
    lanes8 = lax.broadcasted_iota(jnp.int32, (128, 8), 0)
    spread = (lanes8 == lax.broadcasted_iota(jnp.int32, (128, 8), 1) + 16).astype(BF16)
    sib_rows = dot(spread, sib_table[...]).astype(BF16)
    lane = lax.broadcasted_iota(jnp.int32, (RB, 128), 1)
    for b in range(BLOCKS):
        place = lax.broadcasted_iota(jnp.int32, (RB, 1), 0).astype(F32) + (shift + float(b * RB))
        child = (start_row <= place) & (place < end_row)
        chosen = jnp.where(child, 1.0, 0.0).astype(BF16)
        start_of = jnp.sum(jnp.where(child, start_row, 0.0), axis=1, keepdims=True)
        rank = (place - start_of).astype(jnp.int32)
        hot = (rank + 16 == lane).astype(F32).astype(BF16)
        onehot[block(b), :] = hot
        value = (dot(chosen, window[...]) + dot(hot, sib_rows)).astype(BF16)
        inputs[block(b), :] = value
        value = value.astype(F32)
        inverse = lax.rsqrt(jnp.mean(value * value, axis=-1, keepdims=True) + 1e-06)
        inv_in[block(b), :] = inverse
        normed[block(b), :] = (value * inverse * gain[...]).astype(BF16)
    packed[...] = dot(normed[...], w_qkv[...]).astype(BF16)
    for h in range(HEADS):
        states[pl.ds(h * HS, HS), :] = dot_tn(packed[:, head(h, 1)], packed[:, head(h, 2)])

    forward = scan(at, links, states, prefix, f_sib, f_chip, f_z, f_p, f_ret, f_e, f_give, False)
    step(forward)
    for h in range(HEADS):
        for b in range(BLOCKS):
            keys, values = packed[: (b + 1) * RB, head(h, 1)], packed[: (b + 1) * RB, head(h, 2)]
            score = jnp.where(lower(b), dot_nt(packed[block(b), head(h)], keys), 0.0).astype(BF16)
            scores[h, block(b), : (b + 1) * RB] = score
            numer[block(b), head(h)] = dot(score, values)
        step(forward)
    finish(forward)

    for h in range(HEADS):
        high, low = split(prefix[pl.ds(h * HS, HS), :])
        q = packed[:, head(h)]
        wide[:, head(h)] = dot(q, high) + dot(q, low)
    scale = float(DEVS * N) ** (-0.5)
    lane8 = lax.broadcasted_iota(jnp.int32, (RB, 8), 1)
    inv_heads = []
    for b in range(BLOCKS):
        for h in range(HEADS):
            value = numer[block(b), head(h)] + wide[block(b), head(h)]
            numer[block(b), head(h)] = value
            inverse = lax.rsqrt(jnp.mean(value * value, axis=-1, keepdims=True) + 1e-05)
            attended[block(b), head(h)] = (value * inverse).astype(BF16)
            inv_heads.append(inverse)
    wide[...] = dot(attended[...], w_out[...])
    for b in range(BLOCKS):
        value = inputs[block(b), :].astype(F32) + wide[block(b), :]
        resid[block(b), :] = value
        inverse = lax.rsqrt(jnp.mean(value * value, axis=-1, keepdims=True) + 1e-06)
        inv_out[block(b), :] = inverse
        last = (value * inverse).astype(BF16)
        final[block(b), :] = last
        logits = dot(last, w_head[...])
        target = ((occupancy[block(b), :] >> lane8) & 1).astype(F32)
        small_grad = ((jax.nn.sigmoid(logits) - target) * scale).astype(BF16)
        d_logits[block(b), :] = small_grad
        d_final = dot_nt(small_grad, w_head[...])
        mean = jnp.mean(d_final * value, axis=-1, keepdims=True)
        d_value = inverse * d_final - value * (inverse * inverse * inverse) * mean
        d_resid[block(b), :] = d_value
        d_resid_b[block(b), :] = d_value.astype(BF16)
    wide[...] = dot_nt(d_resid_b[...], w_out[...])
    for b in range(BLOCKS):
        for h in range(HEADS):
            piece, value, inverse = wide[block(b), head(h)], numer[block(b), head(h)], inv_heads[b * HEADS + h]
            mean = jnp.mean(piece * value, axis=-1, keepdims=True)
            grads[block(b), head(h)] = (inverse * piece - value * (inverse * inverse * inverse) * mean).astype(BF16)
    for h in range(HEADS):
        qstates[pl.ds(h * HS, HS), :] = dot_tn(packed[:, head(h)], grads[:, head(h)])

    backward = scan(at, links, qstates, suffix, b_sib, b_chip, b_z, b_p, b_ret, b_e, b_give, True)
    step(backward)
    early[:, pl.ds(0, D)] = dot_tn(attended[...], d_resid_b[...])
    step(backward)
    for h in range(HEADS):
        high, low = split(prefix[pl.ds(h * HS, HS), :])
        g = grads[:, head(h)]
        wide[:, head(h)] = dot_nt(g, high) + dot_nt(g, low)
    d_local[...] = jnp.zeros_like(d_local)
    for h in range(HEADS):
        for b in range(BLOCKS):
            upto = pl.ds(0, (b + 1) * RB)
            g, q = grads[block(b), head(h)], packed[block(b), head(h)]
            back = jnp.where(lower(b), dot_nt(g, packed[upto, head(h, 2)]), 0.0).astype(BF16)
            dq = dot(back, packed[upto, head(h, 1)]) + wide[block(b), head(h)]
            d_packed[block(b), head(h)] = dq.astype(BF16)
            d_local[upto, head(h)] += dot_tn(back, q)
            d_local[upto, head(h, 1)] += dot_tn(scores[h, block(b), upto], g)
        if h == 1:
            step(backward)
    early[:, pl.ds(D, D)] = dot_tn(normed[...], d_packed[:, pl.ds(0, D)])
    early_sum = reduce_all(at, links, early, early_out, e_r0, e_r1, e_z, e_r2, e_p)
    step(early_sum)
    wide[...] = dot_nt(d_packed[:, pl.ds(0, D)], w_qkv[:, pl.ds(0, D)])
    step(backward)
    finish(backward)
    step(early_sum)

    for h in range(HEADS):
        high, low = split(suffix[pl.ds(h * HS, HS), :])
        k, v = packed[:, head(h, 1)], packed[:, head(h, 2)]
        d_packed[:, head(h, 1)] = (d_local[:, head(h)] + dot_nt(v, high) + dot_nt(v, low)).astype(BF16)
        d_packed[:, head(h, 2)] = (d_local[:, head(h, 1)] + dot(k, high) + dot(k, low)).astype(BF16)
    late[...] = dot_tn(normed[...], d_packed[:, pl.ds(D, 2 * D)])
    wide[...] += dot_nt(d_packed[:, pl.ds(D, 2 * D)], w_qkv[:, pl.ds(D, 2 * D)])
    step(early_sum)
    grad_gain = jnp.zeros((1, D), F32)
    grad_sib = jnp.zeros((128, D), F32)
    for b in range(BLOCKS):
        value, inverse, slope = inputs[block(b), :].astype(F32), inv_in[block(b), :], wide[block(b), :]
        grad_gain = grad_gain + jnp.sum(slope * value * inverse, axis=0, keepdims=True)
        scaled = slope * gain[...]
        mean = jnp.mean(scaled * value, axis=-1, keepdims=True)
        d_in = inverse * scaled - value * (inverse * inverse * inverse) * mean + d_resid[block(b), :]
        high, low = split(d_in)
        grad_sib = grad_sib + dot_tn(onehot[block(b), :], high) + dot_tn(onehot[block(b), :], low)
    small[pl.ds(0, 8), :] = dot_tn(d_logits[...], final[...])
    small[pl.ds(8, 8), :] = jnp.broadcast_to(grad_gain, (8, D))
    small[pl.ds(16, 16), :] = grad_sib[16:32]
    late_sum = reduce_all(at, links, late, late_out, l_r0, l_r1, l_z, l_r2, l_p, (small, small_out, x0, x1, xz))
    step(late_sum)
    step(early_sum)
    more = True
    while more:
        more = step(late_sum)
        step(early_sum)
    finish(early_sum)
    links.finish()


def vm(shape, dtype=F32):
    return pltpu.VMEM(shape, dtype)


def scan_buffers():
    return [vm((256, HS)), vm((256, HS)), vm((4, 64, HS)), vm((16, 64, HS)), vm((4, 64, HS)), vm((4, 64, HS)), vm((256, HS))]


def sum_buffers(width):
    return [vm((N, 1024)), vm((256, 1024)), vm((256, 1024)), vm((4, 64, 1024)), vm((16, 16, width)), vm((16, 16, width))]


def shards(parent_rows, counts, occupancy, sib_table, gain, w_qkv, w_out, w_head):
    scratch = [
        vm((3 * PAR, D), BF16), vm((3, 16, PAR)), vm((4, 8, 128)), vm((16, 8, 128)), vm((2, 8, 128)),
        vm((N, D), BF16), vm((N, 1)), vm((N, D), BF16), vm((N, 3 * D), BF16), vm((N, 128), BF16),
        vm((HEADS, N, N), BF16), vm((N, D)), vm((N, D)), vm((N, 1)), vm((N, D), BF16), vm((N, D), BF16),
        vm((N, 8), BF16), vm((N, D)), vm((N, D), BF16), vm((N, D)), vm((N, D), BF16), vm((N, 3 * D), BF16),
        vm((N, 2 * D)), vm((N, HS)), vm((N, HS)), vm((N, HS)), vm((N, HS)),
        *scan_buffers(), *scan_buffers(), *sum_buffers(256), *sum_buffers(384),
        vm((32, D)), vm((16, D)), vm((4, 16, 128)), vm((4, 16, 128)),
        pltpu.SemaphoreType.DMA((COPIES,)), pltpu.SemaphoreType.DMA((COPIES,)),
    ]
    spec = pl.BlockSpec(memory_space=pltpu.VMEM)
    early, late, small = pl.pallas_call(
        kernel,
        out_shape=[
            jax.ShapeDtypeStruct((D, 1024), F32),
            jax.ShapeDtypeStruct((D, 1024), F32),
            jax.ShapeDtypeStruct((32, D), F32),
        ],
        in_specs=[spec] * 8,
        out_specs=[spec] * 3,
        scratch_shapes=scratch,
        compiler_params=pltpu.CompilerParams(
            collective_id=0, has_side_effects=True, vmem_limit_bytes=60 * 1024 * 1024
        ),
        name="train_step",
    )(
        parent_rows, counts.reshape(1, PAR), occupancy.reshape(N, 1), sib_table, gain.reshape(1, D),
        w_qkv, w_out, w_head,
    )
    grad_qkv = jnp.concatenate([early[:, D:], late], axis=1)
    return grad_qkv, early[:, :D], small[:8].T, small[8], small[16:24]


def solution(mesh):
    placed = (P("seq", None), P("seq"), P("seq"), P(), P(), P(), P(), P())
    return jax.shard_map(
        shards, mesh=mesh, in_specs=placed, out_specs=(P(), P(), P(), P(), P()), check_vma=False
    )
```

time: 401 us -> 148 us (0.37)
  waiting for transfers between devices: 153 us -> 0 us
  Pallas kernels: 0 us -> 138 us
  blocking collectives: 134 us -> 0 us
  matrix products: 33.5 us -> 0 us
  between operations: 26.2 us -> 0.66 us
  local copies, waits for them, and re-layouts: 25.8 us -> 7.06 us
  starting transfers between devices: 15.5 us -> 0 us
  other arithmetic: 11.1 us -> 1.92 us
    pallas_call x0 -> x1, Pallas kernels: none -> 138 us  [shards(): pl.pallas_call(kernel, out_shape=[jax.ShapeDtypeStruct((D, 1024), F32), j...]
    psum x1 -> x0, waiting for transfers between devices: 83.8 us -> none  [shards(): lax.psum((grad_qkv, grad_out, grad_head, grad_gain, grad_sib), SEQ)]
    psum x1 -> x0, blocking collectives: 72.6 us -> none  [shards(): lax.psum((grad_qkv, grad_out, grad_head, grad_gain, grad_sib), SEQ)]
    all_gather x3 -> x0, waiting for transfers between devices: 66.2 us -> none  [entering(): pieces = lax.all_gather(subtotal, axis)]
    all_gather x5 -> x0, blocking collectives: 37.3 us -> none  [the longest x4 35.1 us: entering_2(): pieces = lax.all_gather(subtotal.astype(jnp.bfloat16), axis)]
    dot_general x59 -> x0, matrix products: 33.5 us -> none  [the longest x4 4.96 us: attend(): jnp.dot(score, values_here.astype(jnp.float32), precision=highest)]
    unnamed x4 -> x0, blocking collectives: 24.6 us -> none
    unnamed x70 -> x5, local copies, waits for them, and re-layouts: 18.7 us -> 1.5 us
  transfers between devices with their start and end apart: 8 -> 0, of which waited for: 5 -> 0; matrix products, arithmetic and copies ran while one was open for 3% -> 0% of each run, Pallas kernels for 0% -> 0%
where the time goes in v1:
time: 148 us; the launch traced here: 147 us
  Pallas kernels  138 us (93%)
  local copies, waits for them, and re-layouts  7.06 us (5%)
  other arithmetic  1.92 us (1%)
    pallas_call x1, Pallas kernels, shards(): pl.pallas_call(kernel, out_shape=[jax.ShapeDtypeStruct((D, 1024), F32), j...  138 us
    slice x3, local copies, waits for them, and re-layouts, shards(): return (grad_qkv, early[:, :D], small[:8].T, small[8], small[16:24])  4.03 us

profile of v1, /device:TPU:1, one launch (start us, length us, event | category | flops | bytes accessed | tf_op | source)
XLA Modules:
  0.0 147.4 jit_solution(14450241245128648657)
XLA Ops:
  0.6 1.5 %copy.15.w_head = bf16[512,8]{1,0:T(8,128)(2,1)} copy(bf16[512,8]{0,1:T(8,128)(2,1)} %param.15) | data formatting | bytes 16384 | tf_op args[7]
  2.1 1.5 %copy.14.occupancy = s32[512,1]{1,0:T(8,128)} copy(s32[512,1]{0,1:T(1,128)} %bitcast.6) | data formatting | bytes 4096 | tf_op jit(solution)/shard_map/reshape | solution.py:463
  3.7 137.8 %train_step.1 = (f32[512,1024]{1,0:T(8,128)}, f32[512,1024]{1,0:T(8,128)}, f32[32,512]{1,0:T(8,128)}) custom-call(bf16[256,512]{1,0:T(8,128)(2,1)} %parents.1, s32[1,256]{1,0:T(1,128)} %bitcast.9, s32[512,1]{1,0:T(8,128)} %copy.14.occupancy, bf16[8,512]{1,0:T(8,128)(2,1)} %sib_table.1, f32[1,512]{1,0:T(1,128)} %bitcast.8, bf16[512,1536]{1,0:T(8,128)(2,1)} %w_qkv.1, ...), custom_call_target="tpu_custom_call" | custom-call | tf_op jit(solution)/shard_map/train_step/pallas_call | solution.py:448
  141.5 0.0 copy-start.1
  141.5 0.0 copy-start
  141.5 2.8 %fusion = (f32[512,512]{1,0:T(8,128)}, f32[512,512]{1,0:T(8,128)S(1)}) fusion(f32[512,1024]{1,0:T(8,128)} %get-tuple-element.8), kind=kLoop, calls=%fused_computation.2 | loop fusion | bytes 4194304 | tf_op jit(solution)/shard_map/slice | solution.py:467
  144.3 0.0 copy-done.1
  144.3 0.6 slice.18
  144.9 0.6 fusion.1
  145.5 0.0 copy-done
  145.5 1.9 %pad_maximum_fusion = f32[512,1536]{1,0:T(8,128)} fusion(f32[512,1024]{1,0:T(8,128)S(1)} %copy-done, f32[512,512]{1,0:T(8,128)S(1)} %get-tuple-element.12), kind=kLoop, calls=%fused_computation | loop fusion | flops 786432 | bytes 6291456 | tf_op jit(solution)/shard_map/concatenate | solution.py:466
Async XLA Ops:
  141.5 2.9 %copy-start.1 = (f32[32,512]{1,0:T(8,128)S(1)}, f32[32,512]{1,0:T(8,128)}, u32[]{:S(2)}) copy-start(f32[32,512]{1,0:T(8,128)} %get-tuple-element.10) | copy-start | bytes 196612
  141.5 4.0 %copy-start = (f32[512,1024]{1,0:T(8,128)S(1)}, f32[512,1024]{1,0:T(8,128)}, u32[]{:S(2)}) copy-start(f32[512,1024]{1,0:T(8,128)} %get-tuple-element.9) | copy-start | bytes 6291460

commit v2 on v1

--- a/solution.py
+++ b/solution.py
@@ -11,7 +11,7 @@
 N, PAR, DEVS = 512, 256, 128
 RB = 128
 BLOCKS = N // RB
-COPIES = 160
+COPIES = 184
 PLANE = [(dx, dy) for dx in range(4) for dy in range(4) if dx or dy]
 
 
@@ -43,6 +43,12 @@
         self.x, self.y, self.z, self.c = me // 32, (me // 8) % 4, (me // 2) % 4, me % 2
         self.g = self.x * 4 + self.y
         self.sibling = me + 1 - 2 * self.c
+        c = self.c
+        self.l, self.l_step = self.z + c * (self.x - self.z), 2 + 30 * c
+        self.p, self.p_step = self.x + c * (self.y - self.x), 32 - 24 * c
+        self.q, self.q_step = self.y + c * (self.z - self.y), 8 - 6 * c
+        self.l_sibling = self.x + c * (self.z - self.x)
+        self.pq = self.p * 4 + self.q
         self.next = (me + 1) % DEVS
         self.prev = (me + DEVS - 1) % DEVS
 
@@ -57,11 +63,22 @@
             yield xt, yt, (xt * 4 + yt) * 8 + self.me % 8
 
 
+    def sum_line(self):
+        for d in (1, 2, 3):
+            lt = (self.l + d) % 4
+            yield lt, self.me + (lt - self.l) * self.l_step
+
+    def sum_plane(self):
+        for dp, dq in PLANE:
+            pt, qt = (self.p + dp) % 4, (self.q + dq) % 4
+            yield pt * 4 + qt, self.me + (pt - self.p) * self.p_step + (qt - self.q) * self.q_step
+
+
 class Links:
     def __init__(self, send, recv):
         self.send, self.recv, self.sent = send, recv, []
 
-    def start(self, src, dst, device):
+    def start(self, src, dst, device, when=None):
         k = len(self.sent)
         copy = pltpu.make_async_remote_copy(
             src_ref=src,
@@ -71,13 +88,19 @@
             device_id=(device,),
             device_id_type=MESH,
         )
-        copy.start()
-        self.sent.append(copy)
+        if when is None:
+            copy.start()
+        else:
+            pl.when(when)(copy.start)
+        self.sent.append((copy, when))
         return copy
 
     def finish(self):
-        for copy in self.sent:
-            copy.wait_send()
+        for copy, when in self.sent:
+            if when is None:
+                copy.wait_send()
+            else:
+                pl.when(when)(copy.wait_send)
 
 
 def arrived(copies):
@@ -90,36 +113,46 @@
     far = at.me + DEVS - 1 + 2 * at.c
     partners = [at.sibling, far % DEVS]
     partners += [dev for zt, dev in at.line()] + [dev for xt, yt, dev in at.plane()]
+    for dy in (1, 2, 3):
+        for zt, dev in at.line():
+            partners.append(dev + (((at.y + dy) % 4) - at.y) * 8)
     for dev in partners:
         pl.semaphore_signal(barrier, inc=1, device_id=(dev,), device_id_type=MESH)
     pl.semaphore_wait(barrier, len(partners))
 
 
-def scan(at, links, state, out, sib, chip, zbuf, pbuf, ret, ebuf, give, reverse):
+def scan(at, links, state, out, sib, mine_c, zbuf, pbuf, ret, ebuf, give, reverse):
     mine, other = rows(at.c * 256, 256), rows((1 - at.c) * 256, 256)
     first = links.start(state.at[other], sib, at.sibling)
     yield
     arrived([first])
-    chip[...] = state[mine, :] + sib[...]
+    chip = state[mine, :] + sib[...]
+    for k in range(4):
+        pack(mine_c.at[k], chip[k * 64 : (k + 1) * 64])
     copies = []
     for zt, dev in at.line():
-        copies.append(links.start(chip.at[rows(zt * 64, 64)], zbuf.at[at.z], dev))
-    zbuf[at.z] = chip[rows(at.z * 64, 64), :]
+        copies.append(links.start(mine_c.at[zt], zbuf.at[at.z], dev))
+    zbuf[at.z] = mine_c[at.z]
     yield
     arrived(copies)
-    pbuf[at.g] = zbuf[0] + zbuf[1] + zbuf[2] + zbuf[3]
+    parts = [unpack(zbuf.at[k]) for k in range(4)]
+    pack(pbuf.at[at.g], parts[0] + parts[1] + parts[2] + parts[3])
     copies = []
-    for xt, yt, dev in at.plane():
-        copies.append(links.start(pbuf.at[at.g], pbuf.at[at.g], dev))
-    yield
-    arrived(copies)
+    for dx, dy in PLANE:
+        gt = ((at.x + dx) % 4) * 4 + (at.y + dy) % 4
+        gs = ((at.x + 4 - dx) % 4) * 4 + (at.y + 4 - dy) % 4
+        goes, comes = (gt < at.g, gs > at.g) if reverse else (gt > at.g, gs < at.g)
+        copies.append((comes, links.start(pbuf.at[at.g], pbuf.at[at.g], gt * 8 + at.me % 8, goes)))
+    yield
+    for comes, copy in copies:
+        pl.when(comes)(copy.wait_recv)
     total = jnp.zeros((64, HS), F32)
     for k in range(16):
         passed = (k > at.g) if reverse else (k < at.g)
-        total = total + jnp.where(passed, pbuf[k], 0.0)
+        total = total + jnp.where(passed, unpack(pbuf.at[k]), 0.0)
     for k in range(3, -1, -1) if reverse else range(4):
-        ret[k] = total
-        total = total + zbuf[k]
+        pack(ret.at[k], total)
+        total = total + parts[k]
     copies = []
     for zt, dev in at.line():
         copies.append(links.start(ret.at[zt], ebuf.at[at.z], dev))
@@ -127,7 +160,7 @@
     yield
     arrived(copies)
     first_core = at.c == (1 if reverse else 0)
-    before = ebuf[...].reshape(256, HS)
+    before = jnp.concatenate([unpack(ebuf.at[k]) for k in range(4)], axis=0)
     give[...] = before + jnp.where(first_core, state[mine, :], 0.0)
     last = links.start(give, out.at[mine], at.sibling)
     out[mine, :] = before + jnp.where(first_core, 0.0, sib[...])
@@ -135,74 +168,167 @@
     arrived([last])
 
 
-def reduce_all(at, links, src, out, r0, r1, zb, r2, pb, small=None):
-    mine, other = rows(at.c * 256, 256), rows((1 - at.c) * 256, 256)
-    copies = [links.start(src.at[other], r0, at.sibling)]
-    if small:
-        xs, xo, x0, x1, xz = small
-        xmine, xother = rows(at.c * 16, 16), rows((1 - at.c) * 16, 16)
-        copies.append(links.start(xs.at[xother], x0, at.sibling))
+def pack(ref, value):
+    codes, exponents = code_of([value])
+    ref[pl.ds(0, 64), :] = codes[0]
+    ref[pl.ds(64, 16), :] = to_i16(jnp.broadcast_to(exponents[0], (16, 128)))
+
+
+def unpack(ref):
+    return number(ref[pl.ds(0, 64), :]) * powers(ref[pl.ds(64, 16), :])[:1]
+
+
+def code_of(blocks):
+    codes, exponents = [], []
+    for value in blocks:
+        most = jnp.max(jnp.abs(value), axis=0, keepdims=True)
+        exponent = jnp.floor(jnp.log2(jnp.maximum(most, 1e-30))) + 1.0
+        codes.append(jnp.round(value * jnp.exp2(14.0 - exponent)).astype(jnp.int32).astype(jnp.int16))
+        exponents.append(exponent)
+    return codes, exponents
+
+
+def powers(tile):
+    return jnp.exp2(tile.astype(jnp.int32).astype(F32) - 14.0)
+
+
+def number(code):
+    return code.astype(jnp.int32).astype(F32)
+
+
+def to_i16(value):
+    return value.astype(jnp.int32).astype(jnp.int16)
+
+
+def reduce_all(at, links, src, r0, own, r1, zb, r2, pb, ag, pa, full):
+    order = [(at.l + d) % 4 for d in (1, 2, 3, 0)]
+    copies = []
+    for d in (1, 2, 3, 0):
+        k = (at.l_sibling + d) % 4
+        copies.append(links.start(src.at[rows((1 - at.c) * 256 + k * 64, 64)], r0.at[k], at.sibling))
+    yield
+    line = []
+    pad = jnp.zeros((8, 128), F32)
+    for i, (lt, dev) in enumerate(at.sum_line()):
+        arrived([copies[i]])
+        blocks = [
+            src[rows(at.c * 256 + lt * 64, 64), pl.ds(j * 128, 128)] + r0[lt, :, pl.ds(j * 128, 128)] for j in range(8)
+        ]
+        codes, exponents = code_of(blocks)
+        for j in range(8):
+            r1[i, pl.ds(j * 64, 64), :] = codes[j]
+        r1[i, pl.ds(512, 16), :] = to_i16(jnp.concatenate(exponents + [pad], axis=0))
+        line.append(links.start(r1.at[i], zb.at[i], dev))
+    arrived([copies[3]])
+    for j in range(8):
+        own[pl.ds(j * 64, 64), :] = (
+            src[rows(at.c * 256 + at.l * 64, 64), pl.ds(j * 128, 128)] + r0[at.l, :, pl.ds(j * 128, 128)]
+        )
+    yield
+    arrived(line)
+    scales = [powers(zb[i, pl.ds(512, 16), :]) for i in range(3)]
+    pad = jnp.zeros((14, 128), F32)
+    for k in range(16):
+        pk, qk = k // 4, k % 4
+        blocks = []
+        for j in (2 * qk, 2 * qk + 1):
+            part = pl.ds(j * 64 + pk * 16, 16)
+            value = own[part, :]
+            for i in range(3):
+                value = value + number(zb[i, part, :]) * scales[i][j : j + 1]
+            blocks.append(value)
+        codes, exponents = code_of(blocks)
+        r2[k, pl.ds(0, 16), :] = codes[0]
+        r2[k, pl.ds(16, 16), :] = codes[1]
+        r2[k, pl.ds(32, 16), :] = to_i16(jnp.concatenate(exponents + [pad], axis=0))
+    plane = []
+    for i, (k, dev) in enumerate(at.sum_plane()):
+        plane.append(links.start(r2.at[k], pb.at[i], dev))
+    yield
+    arrived(plane)
+    scale = powers(r2[at.pq, pl.ds(32, 16), :])
+    total = [number(r2[at.pq, pl.ds(16 * b, 16), :]) * scale[b : b + 1] for b in range(2)]
+    for i in range(15):
+        scale = powers(pb[i, pl.ds(32, 16), :])
+        total = [total[b] + number(pb[i, pl.ds(16 * b, 16), :]) * scale[b : b + 1] for b in range(2)]
+    codes, exponents = code_of(total)
+    row = lax.broadcasted_iota(jnp.int32, (16, 128), 0) - 2 * (at.pq % 8)
+    ag[pl.ds(0, 16), :] = codes[0]
+    ag[pl.ds(16, 16), :] = codes[1]
+    ag[pl.ds(32, 16), :] = to_i16(jnp.where(row == 0, exponents[0], jnp.where(row == 1, exponents[1], 0.0)))
+    plane = []
+    for k, dev in at.sum_plane():
+        plane.append(links.start(ag, pa.at[at.pq], dev))
+    pa[at.pq] = ag[...]
+    yield
+    arrived(plane)
+    mine = full.at[at.c, at.l]
+    for k in range(16):
+        mine[pl.ds(k * 32, 32), :] = pa[k, pl.ds(0, 32), :]
+    for b in range(2):
+        tile = pa[8 * b, pl.ds(32, 16), :].astype(jnp.int32)
+        for k in range(1, 8):
+            tile = tile + pa[8 * b + k, pl.ds(32, 16), :].astype(jnp.int32)
+        mine[pl.ds(512 + 16 * b, 16), :] = tile.astype(jnp.int16)
+    line = []
+    for lt, dev in at.sum_line():
+        line.append(links.start(mine, mine, dev))
+    other = [links.start(mine, mine, at.sibling)]
+    yield
+    for d in (1, 2, 3):
+        arrived([line[d - 1]])
+        k = (at.l + 4 - d) % 4
+        other.append(links.start(full.at[at.c, k], full.at[at.c, k], at.sibling))
+    yield
+    arrived(other)
+
+
+def decode(early, late, small, qkv_out, out_out, head_out, gain_out, sib_out):
+    for full, first in ((early, 0), (late, 1024)):
+        scales = [powers(full[0, 0, pl.ds(512 + 16 * b, 16), :]) for b in range(2)]
+        for g in range(16):
+            for b in range(2):
+                e = 2 * (g % 8) + b
+                value = number(full[0, 0, pl.ds(g * 32 + b * 16, 16), :]) * scales[g // 8][e : e + 1]
+                column = first + (g % 4) * 256 + b * 128
+                out, column = (out_out, column) if column < D else (qkv_out, column - D)
+                out[pl.ds(g // 4 * 16, 16), pl.ds(column, 128)] = value
+    head_out[...] = small[pl.ds(0, 8), :]
+    gain_out[...] = small[pl.ds(8, 1), :]
+    sib_out[...] = small[pl.ds(16, 8), :]
+
+
+def reduce_small(at, links, xs, xo, x0, x1, xz, xp):
+    mine, other = rows(at.c * 16, 16), rows((1 - at.c) * 16, 16)
+    first = links.start(xs.at[other], x0, at.sibling)
+    yield
+    arrived([first])
+    total = xs[mine, :] + x0[...]
+    for k in range(4):
+        x1[k] = total[:, k * 128 : (k + 1) * 128]
+    copies = []
+    for lt, dev in at.sum_line():
+        copies.append(links.start(x1.at[lt], xz.at[at.l], dev))
+    xz[at.l] = x1[at.l]
     yield
     arrived(copies)
-    for k in range(4):
-        part = pl.ds(k * 64, 64)
-        r1[part, :] = src[rows(at.c * 256 + k * 64, 64), :] + r0[part, :]
+    xp[at.pq] = xz[0] + xz[1] + xz[2] + xz[3]
     copies = []
-    if small:
-        total = xs[xmine, :] + x0[...]
-        for k in range(4):
-            x1[k] = total[:, k * 128 : (k + 1) * 128]
-        for zt, dev in at.line():
-            copies.append(links.start(x1.at[zt], xz.at[at.z], dev))
-        xz[at.z] = x1[at.z]
-    for zt, dev in at.line():
-        copies.append(links.start(r1.at[rows(zt * 64, 64)], zb.at[at.z], dev))
+    for k, dev in at.sum_plane():
+        copies.append(links.start(xp.at[at.pq], xp.at[at.pq], dev))
     yield
     arrived(copies)
-    width = 384 if small else 256
-    own = at.z * 64
-    for k in range(16):
-        xk, yk = k // 4, k % 4
-        cols = pl.ds(yk * 256, 256)
-        value = jnp.zeros((16, 256), F32)
-        for j in range(4):
-            piece = jnp.where(j == at.z, r1[rows(own + xk * 16, 16), cols], zb[j, pl.ds(xk * 16, 16), cols])
-            value = value + piece
-        r2[k, :, pl.ds(0, 256)] = value
-    if small:
-        value = xz[0] + xz[1] + xz[2] + xz[3]
-        for k in range(16):
-            r2[k, :, pl.ds(256, 128)] = value
+    total = xp[0]
+    for k in range(1, 16):
+        total = total + xp[k]
+    place = xo.at[mine, rows(at.l * 128, 128)]
+    place[...] = total
     copies = []
-    for xt, yt, dev in at.plane():
-        copies.append(links.start(r2.at[xt * 4 + yt], pb.at[at.g], dev))
-    pb[at.g] = r2[at.g]
+    for lt, dev in at.sum_line():
+        copies.append(links.start(place, place, dev))
     yield
     arrived(copies)
-    total = pb[0]
-    for k in range(1, 16):
-        total = total + pb[k]
-    place = out.at[rows(at.c * 256 + own + at.x * 16, 16), rows(at.y * 256, 256)]
-    place[...] = total[:, :256]
-    copies = []
-    for xt, yt, dev in at.plane():
-        copies.append(links.start(place, place, dev))
-    if small:
-        xplace = xo.at[xmine, rows(at.z * 128, 128)]
-        xplace[...] = total[:, 256:]
-        for zt, dev in at.line():
-            copies.append(links.start(xplace, xplace, dev))
-    yield
-    arrived(copies)
-    place = out.at[rows(at.c * 256 + own, 64)]
-    copies = []
-    for zt, dev in at.line():
-        copies.append(links.start(place, place, dev))
-    if small:
-        copies.append(links.start(xo.at[xmine], xo.at[xmine], at.sibling))
-    yield
-    arrived(copies)
-    last = links.start(out.at[mine], out.at[mine], at.sibling)
+    last = links.start(xo.at[mine], xo.at[mine], at.sibling)
     yield
     arrived([last])
 
@@ -233,45 +359,52 @@
 
 
 def kernel(
-    parents, counts, occupancy, sib_table, gain, w_qkv, w_out, w_head,
-    early_out, late_out, small_out,
+    parents, counts_in, occupancy_in, sib_in, gain_in, w_qkv_in, w_out_in, w_head_in,
+    e_full, l_full, small_out,
     window, ends, offz, offp, offs, inputs, inv_in, normed, packed, onehot,
     scores, numer, resid, inv_out, final, attended, d_logits, d_resid, d_resid_b, wide, grads, d_packed,
     d_local, states, prefix, qstates, suffix,
     f_sib, f_chip, f_z, f_p, f_ret, f_e, f_give,
     b_sib, b_chip, b_z, b_p, b_ret, b_e, b_give,
-    early, e_r0, e_r1, e_z, e_r2, e_p,
-    late, l_r0, l_r1, l_z, l_r2, l_p,
-    small, x0, x1, xz,
-    send, recv,
+    early, e_r0, e_own, e_r1, e_z, e_r2, e_p, e_ag, e_pa,
+    late, l_r0, l_own, l_r1, l_z, l_r2, l_p, l_ag, l_pa,
+    small, x0, x1, xz, xp,
+    counts, occupancy, sib_table, gain, w_qkv, w_out, w_head,
+    send, recv, load,
 ):
     at = Place()
     links = Links(send, recv)
+    own = pl.ds(PAR, PAR)
+    pairs = [
+        (counts_in, counts), (parents, window.at[own]), (sib_in, sib_table), (gain_in, gain), (w_qkv_in, w_qkv),
+        (occupancy_in, occupancy), (w_out_in, w_out), (w_head_in, w_head),
+    ]
+    loads = [pltpu.make_async_copy(src, dst, load.at[i]) for i, (src, dst) in enumerate(pairs)]
+    for copy in loads:
+        copy.start()
     greet(at)
 
-    own = pl.ds(PAR, PAR)
+    loads[0].wait()
+    count = jnp.broadcast_to(counts[...].astype(F32), (16, PAR))
+    whole = jnp.sum(count[:8], axis=1, keepdims=True)
+    offs[0] = jnp.broadcast_to(whole, (8, 128))
+    first = links.start(offs.at[0], offs.at[1], at.sibling)
     tri = (
         lax.broadcasted_iota(jnp.int32, (PAR, PAR), 0) <= lax.broadcasted_iota(jnp.int32, (PAR, PAR), 1)
     ).astype(BF16)
-    count = jnp.broadcast_to(counts[...].astype(F32), (16, PAR))
     local_ends = dot(count.astype(BF16), tri)[:8]
-    whole = jnp.sum(count[:8], axis=1, keepdims=True)
     ends[1, :8] = local_ends
     ends[1, 8:] = count[:8]
+    arrived([first])
+    offset = jnp.where(at.c == 1, offs[1], 0.0)
+    offz[at.z] = offs[0] + offs[1]
+    copies = [links.start(offz.at[at.z], offz.at[at.z], dev) for zt, dev in at.line()]
     halo = [
         links.start(ends.at[1], ends.at[0], at.next),
         links.start(ends.at[1], ends.at[2], at.prev),
         links.start(parents, window.at[pl.ds(0, PAR)], at.next),
         links.start(parents, window.at[pl.ds(2 * PAR, PAR)], at.prev),
     ]
-    window[own, :] = parents[...]
-
-    offs[0] = jnp.broadcast_to(whole, (8, 128))
-    first = links.start(offs.at[0], offs.at[1], at.sibling)
-    arrived([first])
-    offset = jnp.where(at.c == 1, offs[1], 0.0)
-    offz[at.z] = offs[0] + offs[1]
-    copies = [links.start(offz.at[at.z], offz.at[at.z], dev) for zt, dev in at.line()]
     arrived(copies)
     offp[at.g] = offz[0] + offz[1] + offz[2] + offz[3]
     copies = [links.start(offp.at[at.g], offp.at[at.g], dev) for xt, yt, dev in at.plane()]
@@ -283,6 +416,8 @@
     shift = (at.me * N).astype(F32) - offset[:1, :1]
 
     arrived(halo)
+    for copy in loads[1:]:
+        copy.wait()
     own_total = whole[:1, :1]
     low_total = ends[0, :1, PAR - 1 :]
     end_row = jnp.concatenate([ends[0, :1] - low_total, local_ends[:1], ends[2, :1] + own_total], axis=1)
@@ -327,6 +462,7 @@
         wide[:, head(h)] = dot(q, high) + dot(q, low)
     scale = float(DEVS * N) ** (-0.5)
     lane8 = lax.broadcasted_iota(jnp.int32, (RB, 8), 1)
+    symbols = jnp.broadcast_to(occupancy[...].astype(F32), (8, N)).T.astype(jnp.int32)
     inv_heads = []
     for b in range(BLOCKS):
         for h in range(HEADS):
@@ -343,11 +479,11 @@
         inv_out[block(b), :] = inverse
         last = (value * inverse).astype(BF16)
         final[block(b), :] = last
-        logits = dot(last, w_head[...])
-        target = ((occupancy[block(b), :] >> lane8) & 1).astype(F32)
+        logits = dot_nt(last, w_head[...])
+        target = ((symbols[b * RB : (b + 1) * RB] >> lane8) & 1).astype(F32)
         small_grad = ((jax.nn.sigmoid(logits) - target) * scale).astype(BF16)
         d_logits[block(b), :] = small_grad
-        d_final = dot_nt(small_grad, w_head[...])
+        d_final = dot(small_grad, w_head[...])
         mean = jnp.mean(d_final * value, axis=-1, keepdims=True)
         d_value = inverse * d_final - value * (inverse * inverse * inverse) * mean
         d_resid[block(b), :] = d_value
@@ -381,13 +517,14 @@
             d_local[upto, head(h, 1)] += dot_tn(scores[h, block(b), upto], g)
         if h == 1:
             step(backward)
+    step(backward)
     early[:, pl.ds(D, D)] = dot_tn(normed[...], d_packed[:, pl.ds(0, D)])
-    early_sum = reduce_all(at, links, early, early_out, e_r0, e_r1, e_z, e_r2, e_p)
+    early_sum = reduce_all(at, links, early, e_r0, e_own, e_r1, e_z, e_r2, e_p, e_ag, e_pa, e_full)
     step(early_sum)
     wide[...] = dot_nt(d_packed[:, pl.ds(0, D)], w_qkv[:, pl.ds(0, D)])
     step(backward)
+    step(early_sum)
     finish(backward)
-    step(early_sum)
 
     for h in range(HEADS):
         high, low = split(suffix[pl.ds(h * HS, HS), :])
@@ -395,8 +532,11 @@
         d_packed[:, head(h, 1)] = (d_local[:, head(h)] + dot_nt(v, high) + dot_nt(v, low)).astype(BF16)
         d_packed[:, head(h, 2)] = (d_local[:, head(h, 1)] + dot(k, high) + dot(k, low)).astype(BF16)
     late[...] = dot_tn(normed[...], d_packed[:, pl.ds(D, 2 * D)])
+    late_sum = reduce_all(at, links, late, l_r0, l_own, l_r1, l_z, l_r2, l_p, l_ag, l_pa, l_full)
+    step(late_sum)
+    step(early_sum)
+    step(late_sum)
     wide[...] += dot_nt(d_packed[:, pl.ds(D, 2 * D)], w_qkv[:, pl.ds(D, 2 * D)])
-    step(early_sum)
     grad_gain = jnp.zeros((1, D), F32)
     grad_sib = jnp.zeros((128, D), F32)
     for b in range(BLOCKS):
@@ -410,14 +550,16 @@
     small[pl.ds(0, 8), :] = dot_tn(d_logits[...], final[...])
     small[pl.ds(8, 8), :] = jnp.broadcast_to(grad_gain, (8, D))
     small[pl.ds(16, 16), :] = grad_sib[16:32]
-    late_sum = reduce_all(at, links, late, late_out, l_r0, l_r1, l_z, l_r2, l_p, (small, small_out, x0, x1, xz))
-    step(late_sum)
+    small_sum = reduce_small(at, links, small, small_out, x0, x1, xz, xp)
+    step(small_sum)
     step(early_sum)
     more = True
     while more:
+        step(small_sum)
         more = step(late_sum)
         step(early_sum)
     finish(early_sum)
+    finish(small_sum)
     links.finish()
 
 
@@ -426,11 +568,16 @@
 
 
 def scan_buffers():
-    return [vm((256, HS)), vm((256, HS)), vm((4, 64, HS)), vm((16, 64, HS)), vm((4, 64, HS)), vm((4, 64, HS)), vm((256, HS))]
-
-
-def sum_buffers(width):
-    return [vm((N, 1024)), vm((256, 1024)), vm((256, 1024)), vm((4, 64, 1024)), vm((16, 16, width)), vm((16, 16, width))]
+    coded = [vm((k, 80, 128), jnp.int16) for k in (4, 4, 16, 4, 4)]
+    return [vm((256, HS)), *coded, vm((256, HS))]
+
+
+def sum_buffers():
+    i16 = jnp.int16
+    return [
+        vm((N, 1024)), vm((4, 64, 1024)), vm((512, 128)), vm((3, 528, 128), i16), vm((3, 528, 128), i16),
+        vm((16, 48, 128), i16), vm((15, 48, 128), i16), vm((48, 128), i16), vm((16, 48, 128), i16),
+    ]
 
 
 def shards(parent_rows, counts, occupancy, sib_table, gain, w_qkv, w_out, w_head):
@@ -440,31 +587,43 @@
         vm((HEADS, N, N), BF16), vm((N, D)), vm((N, D)), vm((N, 1)), vm((N, D), BF16), vm((N, D), BF16),
         vm((N, 8), BF16), vm((N, D)), vm((N, D), BF16), vm((N, D)), vm((N, D), BF16), vm((N, 3 * D), BF16),
         vm((N, 2 * D)), vm((N, HS)), vm((N, HS)), vm((N, HS)), vm((N, HS)),
-        *scan_buffers(), *scan_buffers(), *sum_buffers(256), *sum_buffers(384),
-        vm((32, D)), vm((16, D)), vm((4, 16, 128)), vm((4, 16, 128)),
-        pltpu.SemaphoreType.DMA((COPIES,)), pltpu.SemaphoreType.DMA((COPIES,)),
+        *scan_buffers(), *scan_buffers(), *sum_buffers(), *sum_buffers(),
+        vm((32, D)), vm((16, D)), vm((4, 16, 128)), vm((4, 16, 128)), vm((16, 16, 128)),
+        vm((1, PAR), jnp.int32), vm((1, N), jnp.int32), vm((8, D), BF16), vm((1, D)), vm((D, 3 * D), BF16), vm((D, D), BF16),
+        vm((8, D), BF16),
+        pltpu.SemaphoreType.DMA((COPIES,)), pltpu.SemaphoreType.DMA((COPIES,)), pltpu.SemaphoreType.DMA((8,)),
     ]
     spec = pl.BlockSpec(memory_space=pltpu.VMEM)
+    codes = jax.ShapeDtypeStruct((2, 4, 544, 128), jnp.int16)
     early, late, small = pl.pallas_call(
         kernel,
-        out_shape=[
-            jax.ShapeDtypeStruct((D, 1024), F32),
-            jax.ShapeDtypeStruct((D, 1024), F32),
-            jax.ShapeDtypeStruct((32, D), F32),
-        ],
-        in_specs=[spec] * 8,
+        out_shape=[codes, codes, jax.ShapeDtypeStruct((32, D), F32)],
+        in_specs=[pl.BlockSpec(memory_space=pltpu.HBM)] * 8,
         out_specs=[spec] * 3,
         scratch_shapes=scratch,
         compiler_params=pltpu.CompilerParams(
-            collective_id=0, has_side_effects=True, vmem_limit_bytes=60 * 1024 * 1024
+            collective_id=0, has_side_effects=True, vmem_limit_bytes=58 * 1024 * 1024
         ),
         name="train_step",
     )(
-        parent_rows, counts.reshape(1, PAR), occupancy.reshape(N, 1), sib_table, gain.reshape(1, D),
-        w_qkv, w_out, w_head,
+        parent_rows, counts.reshape(1, PAR), occupancy.reshape(1, N), sib_table, gain.reshape(1, D),
+        w_qkv, w_out, w_head.T,
     )
-    grad_qkv = jnp.concatenate([early[:, D:], late], axis=1)
-    return grad_qkv, early[:, :D], small[:8].T, small[8], small[16:24]
+    piece = pl.BlockSpec((1, 1, 544, 128), lambda i: (i // 4, i % 4, 0, 0))
+    whole = [(8, D), (1, D), (8, D)]
+    grad_qkv, grad_out, grad_head, grad_gain, grad_sib = pl.pallas_call(
+        decode,
+        grid=(8,),
+        in_specs=[piece, piece, pl.BlockSpec((32, D), lambda i: (0, 0))],
+        out_specs=[
+            pl.BlockSpec((64, 3 * D), lambda i: (i, 0)),
+            pl.BlockSpec((64, D), lambda i: (i, 0)),
+            *[pl.BlockSpec(shape, lambda i: (0, 0)) for shape in whole],
+        ],
+        out_shape=[jax.ShapeDtypeStruct(shape, F32) for shape in [(D, 3 * D), (D, D), *whole]],
+        name="decode",
+    )(early, late, small)
+    return grad_qkv, grad_out, grad_head.T, grad_gain.reshape(D), grad_sib
 
 
 def solution(mesh):

time: 148 us -> 103 us (0.70)
  Pallas kernels: 138 us -> 102 us
  local copies, waits for them, and re-layouts: 7.06 us -> 0 us
  other arithmetic: 1.92 us -> 0 us
    pallas_call x1 -> x2, Pallas kernels: 138 us -> 102 us  [the longest x1 95.7 us: shards(): pl.pallas_call(kernel, out_shape=[codes, codes, jax.ShapeDtypeStruct((32,...]
    slice x3 -> x0, local copies, waits for them, and re-layouts: 4.03 us -> none  [shards(): return (grad_qkv, early[:, :D], small[:8].T, small[8], small[16:24])]
    concatenate x1 -> x0, other arithmetic: 1.92 us -> none  [shards(): grad_qkv = jnp.concatenate([early[:, D:], late], axis=1)]
    reshape x1 -> x0, local copies, waits for them, and re-layouts: 1.53 us -> none  [shards(): occupancy.reshape(N, 1)]
    unnamed x5 -> x0, local copies, waits for them, and re-layouts: 1.5 us -> none
where the time goes in v2:
time: 103 us
  Pallas kernels  102 us (99%)
    pallas_call x1, Pallas kernels, shards(): pl.pallas_call(kernel, out_shape=[codes, codes, jax.ShapeDtypeStruct((32,...  95.7 us
    pallas_call x1, Pallas kernels, shards(): pl.pallas_call(decode, grid=(8,), in_specs=[piece, piece, pl.BlockSpec((3...  6.33 us

profile of v2, /device:TPU:1, one launch (start us, length us, event | category | flops | bytes accessed | tf_op | source)
XLA Modules:
  0.0 102.6 jit_solution(3185620478190657265)
XLA Ops:
  0.6 95.7 %train_step.1 = (s16[2,4,544,128]{3,2,1,0:T(8,128)(2,1)}, s16[2,4,544,128]{3,2,1,0:T(8,128)(2,1)}, f32[32,512]{1,0:T(8,128)}) custom-call(bf16[256,512]{1,0:T(8,128)(2,1)} %parents.1, s32[1,256]{1,0:T(1,128)} %bitcast.9, s32[1,512]{1,0:T(1,128)} %bitcast.7, bf16[8,512]{1,0:T(8,128)(2,1)} %sib_in.1, f32[1,512]{1,0:T(1,128)} %bitcast.8, ...), custom_call_target="tpu_custom_call" | custom-call | tf_op jit(solution)/shard_map/train_step/pallas_call | solution.py:598
  96.3 6.3 %decode.1 = (f32[512,1536]{1,0:T(8,128)}, f32[512,512]{1,0:T(8,128)}, f32[8,512]{1,0:T(8,128)}, f32[1,512]{1,0:T(1,128)}, f32[8,512]{1,0:T(8,128)}) custom-call(s16[2,4,544,128]{3,2,1,0:T(8,128)(2,1)} %get-tuple-element.13.early, s16[2,4,544,128]{3,2,1,0:T(8,128)(2,1)} %get-tuple-element.14.late, f32[32,512]{1,0:T(8,128)} %get-tuple-element.15.small), custom_call_target="tpu_custom_call" | custom-call | tf_op jit(solution)/shard_map/decode/pallas_call | solution.py:614

commit v3 on v2

--- a/solution.py
+++ b/solution.py
@@ -118,7 +118,7 @@
             partners.append(dev + (((at.y + dy) % 4) - at.y) * 8)
     for dev in partners:
         pl.semaphore_signal(barrier, inc=1, device_id=(dev,), device_id_type=MESH)
-    pl.semaphore_wait(barrier, len(partners))
+    return lambda: pl.semaphore_wait(barrier, len(partners))
 
 
 def scan(at, links, state, out, sib, mine_c, zbuf, pbuf, ret, ebuf, give, reverse):
@@ -283,19 +283,32 @@
     arrived(other)
 
 
-def decode(early, late, small, qkv_out, out_out, head_out, gain_out, sib_out):
-    for full, first in ((early, 0), (late, 1024)):
-        scales = [powers(full[0, 0, pl.ds(512 + 16 * b, 16), :]) for b in range(2)]
-        for g in range(16):
-            for b in range(2):
-                e = 2 * (g % 8) + b
-                value = number(full[0, 0, pl.ds(g * 32 + b * 16, 16), :]) * scales[g // 8][e : e + 1]
-                column = first + (g % 4) * 256 + b * 128
-                out, column = (out_out, column) if column < D else (qkv_out, column - D)
-                out[pl.ds(g // 4 * 16, 16), pl.ds(column, 128)] = value
+def decode(early_in, late_in, small, qkv_out, out_out, head_out, gain_out, sib_out, early, late, qkv, out, load, store):
+    loads, stores = [], []
+    for k in range(8):
+        for i, (src, dst) in enumerate(((early_in, early), (late_in, late))):
+            loads.append(pltpu.make_async_copy(src.at[k // 4, k % 4], dst.at[k], load.at[2 * k + i]))
+            loads[-1].start()
+    for k in range(8):
+        for i, (full, first) in enumerate(((early, 0), (late, 1024))):
+            loads[2 * k + i].wait()
+            scales = [powers(full[k, pl.ds(512 + 16 * b, 16), :]) for b in range(2)]
+            for g in range(16):
+                for b in range(2):
+                    e = 2 * (g % 8) + b
+                    value = number(full[k, pl.ds(g * 32 + b * 16, 16), :]) * scales[g // 8][e : e + 1]
+                    column = first + (g % 4) * 256 + b * 128
+                    to, column = (out, column) if column < D else (qkv, column - D)
+                    to[pl.ds(k * 64 + g // 4 * 16, 16), pl.ds(column, 128)] = value
+        part = pl.ds(k * 64, 64)
+        for i, (src, dst) in enumerate(((qkv, qkv_out), (out, out_out))):
+            stores.append(pltpu.make_async_copy(src.at[part], dst.at[part], store.at[2 * k + i]))
+            stores[-1].start()
     head_out[...] = small[pl.ds(0, 8), :]
     gain_out[...] = small[pl.ds(8, 1), :]
     sib_out[...] = small[pl.ds(16, 8), :]
+    for copy in stores:
+        copy.wait()
 
 
 def reduce_small(at, links, xs, xo, x0, x1, xz, xp):
@@ -369,7 +382,7 @@
     early, e_r0, e_own, e_r1, e_z, e_r2, e_p, e_ag, e_pa,
     late, l_r0, l_own, l_r1, l_z, l_r2, l_p, l_ag, l_pa,
     small, x0, x1, xz, xp,
-    counts, occupancy, sib_table, gain, w_qkv, w_out, w_head,
+    counts, occupancy, sib_table, gain, w_qkv, w_out, w_head, pair_rows, pair_kv, moved,
     send, recv, load,
 ):
     at = Place()
@@ -382,23 +395,40 @@
     loads = [pltpu.make_async_copy(src, dst, load.at[i]) for i, (src, dst) in enumerate(pairs)]
     for copy in loads:
         copy.start()
-    greet(at)
+    all_here = greet(at)
 
     loads[0].wait()
     count = jnp.broadcast_to(counts[...].astype(F32), (16, PAR))
     whole = jnp.sum(count[:8], axis=1, keepdims=True)
     offs[0] = jnp.broadcast_to(whole, (8, 128))
-    first = links.start(offs.at[0], offs.at[1], at.sibling)
     tri = (
         lax.broadcasted_iota(jnp.int32, (PAR, PAR), 0) <= lax.broadcasted_iota(jnp.int32, (PAR, PAR), 1)
     ).astype(BF16)
     local_ends = dot(count.astype(BF16), tri)[:8]
     ends[1, :8] = local_ends
     ends[1, 8:] = count[:8]
+    count_col = count[:8].T[:, :1]
+    start_col = (local_ends - count[:8]).T[:, :1]
+    for copy in loads[1:]:
+        copy.wait()
+    for r in range(8):
+        value = (window[own, :].astype(F32) + sib_table[r : r + 1, :].astype(F32)).astype(BF16).astype(F32)
+        inverse = lax.rsqrt(jnp.mean(value * value, axis=-1, keepdims=True) + 1e-06)
+        inverse = jnp.where(count_col > float(r), inverse, 0.0)
+        pair_rows[pl.ds(r * PAR, PAR), :] = (value * inverse * gain[...]).astype(BF16)
+    pair_kv[...] = dot(pair_rows[...], w_qkv[:, pl.ds(D, 2 * D)]).astype(BF16)
+    for h in range(HEADS):
+        states[pl.ds(h * HS, HS), :] = dot_tn(pair_kv[:, head(h)], pair_kv[:, head(h, 1)])
+    all_here()
+
+    first = links.start(offs.at[0], offs.at[1], at.sibling)
+    forward = scan(at, links, states, prefix, f_sib, f_chip, f_z, f_p, f_ret, f_e, f_give, False)
+    step(forward)
     arrived([first])
     offset = jnp.where(at.c == 1, offs[1], 0.0)
     offz[at.z] = offs[0] + offs[1]
     copies = [links.start(offz.at[at.z], offz.at[at.z], dev) for zt, dev in at.line()]
+    step(forward)
     halo = [
         links.start(ends.at[1], ends.at[0], at.next),
         links.start(ends.at[1], ends.at[2], at.prev),
@@ -410,14 +440,13 @@
     copies = [links.start(offp.at[at.g], offp.at[at.g], dev) for xt, yt, dev in at.plane()]
     for k in range(4):
         offset = offset + jnp.where(k < at.z, offz[k], 0.0)
+    step(forward)
     arrived(copies)
     for k in range(16):
         offset = offset + jnp.where(k < at.g, offp[k], 0.0)
     shift = (at.me * N).astype(F32) - offset[:1, :1]
-
     arrived(halo)
-    for copy in loads[1:]:
-        copy.wait()
+
     own_total = whole[:1, :1]
     low_total = ends[0, :1, PAR - 1 :]
     end_row = jnp.concatenate([ends[0, :1] - low_total, local_ends[:1], ends[2, :1] + own_total], axis=1)
@@ -442,19 +471,28 @@
         inv_in[block(b), :] = inverse
         normed[block(b), :] = (value * inverse * gain[...]).astype(BF16)
     packed[...] = dot(normed[...], w_qkv[...]).astype(BF16)
-    for h in range(HEADS):
-        states[pl.ds(h * HS, HS), :] = dot_tn(packed[:, head(h, 1)], packed[:, head(h, 2)])
-
-    forward = scan(at, links, states, prefix, f_sib, f_chip, f_z, f_p, f_ret, f_e, f_give, False)
     step(forward)
+
     for h in range(HEADS):
         for b in range(BLOCKS):
             keys, values = packed[: (b + 1) * RB, head(h, 1)], packed[: (b + 1) * RB, head(h, 2)]
             score = jnp.where(lower(b), dot_nt(packed[block(b), head(h)], keys), 0.0).astype(BF16)
             scores[h, block(b), : (b + 1) * RB] = score
             numer[block(b), head(h)] = dot(score, values)
-        step(forward)
+        if h == 2:
+            step(forward)
+    for r in range(8):
+        part = pl.ds(r * PAR, PAR)
+        before = jnp.where(start_col + float(r) < shift, 1.0, 0.0)
+        pair_rows[part, :] = (pair_kv[part, pl.ds(0, D)].astype(F32) * before).astype(BF16)
+    place = lax.broadcasted_iota(jnp.int32, (N, 1), 0).astype(F32) + shift
+    wide[...] = packed[:, pl.ds(D, D)].astype(F32) * jnp.where(place < 0.0, -1.0, 0.0)
+    for h in range(HEADS):
+        moved[pl.ds(h * HS, HS), :] = dot_tn(pair_rows[:, head(h)], pair_kv[:, head(h, 1)]) + dot_tn(
+            wide[:, head(h)].astype(BF16), packed[:, head(h, 2)]
+        )
     finish(forward)
+    prefix[...] += moved[...]
 
     for h in range(HEADS):
         high, low = split(prefix[pl.ds(h * HS, HS), :])
@@ -590,7 +628,7 @@
         *scan_buffers(), *scan_buffers(), *sum_buffers(), *sum_buffers(),
         vm((32, D)), vm((16, D)), vm((4, 16, 128)), vm((4, 16, 128)), vm((16, 16, 128)),
         vm((1, PAR), jnp.int32), vm((1, N), jnp.int32), vm((8, D), BF16), vm((1, D)), vm((D, 3 * D), BF16), vm((D, D), BF16),
-        vm((8, D), BF16),
+        vm((8, D), BF16), vm((8 * PAR, D), BF16), vm((8 * PAR, 2 * D), BF16), vm((N, HS)),
         pltpu.SemaphoreType.DMA((COPIES,)), pltpu.SemaphoreType.DMA((COPIES,)), pltpu.SemaphoreType.DMA((8,)),
     ]
     spec = pl.BlockSpec(memory_space=pltpu.VMEM)
@@ -609,18 +647,18 @@
         parent_rows, counts.reshape(1, PAR), occupancy.reshape(1, N), sib_table, gain.reshape(1, D),
         w_qkv, w_out, w_head.T,
     )
-    piece = pl.BlockSpec((1, 1, 544, 128), lambda i: (i // 4, i % 4, 0, 0))
-    whole = [(8, D), (1, D), (8, D)]
+    hbm = pl.BlockSpec(memory_space=pl.ANY)
+    shapes = [(D, 3 * D), (D, D), (8, D), (1, D), (8, D)]
     grad_qkv, grad_out, grad_head, grad_gain, grad_sib = pl.pallas_call(
         decode,
-        grid=(8,),
-        in_specs=[piece, piece, pl.BlockSpec((32, D), lambda i: (0, 0))],
-        out_specs=[
-            pl.BlockSpec((64, 3 * D), lambda i: (i, 0)),
-            pl.BlockSpec((64, D), lambda i: (i, 0)),
-            *[pl.BlockSpec(shape, lambda i: (0, 0)) for shape in whole],
+        in_specs=[hbm, hbm, spec],
+        out_specs=[hbm, hbm, spec, spec, spec],
+        out_shape=[jax.ShapeDtypeStruct(shape, F32) for shape in shapes],
+        scratch_shapes=[
+            vm((8, 544, 128), jnp.int16), vm((8, 544, 128), jnp.int16), vm((D, 3 * D)), vm((D, D)),
+            pltpu.SemaphoreType.DMA((16,)), pltpu.SemaphoreType.DMA((16,)),
         ],
-        out_shape=[jax.ShapeDtypeStruct(shape, F32) for shape in [(D, 3 * D), (D, D), *whole]],
+        compiler_params=pltpu.CompilerParams(vmem_limit_bytes=58 * 1024 * 1024),
         name="decode",
     )(early, late, small)
     return grad_qkv, grad_out, grad_head.T, grad_gain.reshape(D), grad_sib

time: 103 us -> 96.2 us (0.934)
  Pallas kernels: 102 us -> 95.1 us
    pallas_call x1, Pallas kernels: 95.7 us -> 90.4 us  [shards(): pl.pallas_call(kernel, out_shape=[codes, codes, jax.ShapeDtypeStruct((32,...]
    pallas_call x1, Pallas kernels: 6.33 us -> 4.73 us  [shards(): pl.pallas_call(decode, in_specs=[hbm, hbm, spec], out_specs=[hbm, hbm, sp...]
where the time goes in v3:
time: 96.2 us; the launch traced here: 95.9 us
  Pallas kernels  95.1 us (99%)
    pallas_call x1, Pallas kernels, shards(): pl.pallas_call(kernel, out_shape=[codes, codes, jax.ShapeDtypeStruct((32,...  90.4 us
    pallas_call x1, Pallas kernels, shards(): pl.pallas_call(decode, in_specs=[hbm, hbm, spec], out_specs=[hbm, hbm, sp...  4.73 us

profile of v3, /device:TPU:1, one launch (start us, length us, event | category | flops | bytes accessed | tf_op | source)
XLA Modules:
  0.0 95.9 jit_solution(15482936628333375087)
XLA Ops:
  0.6 90.4 %train_step.1 = (s16[2,4,544,128]{3,2,1,0:T(8,128)(2,1)}, s16[2,4,544,128]{3,2,1,0:T(8,128)(2,1)}, f32[32,512]{1,0:T(8,128)}) custom-call(bf16[256,512]{1,0:T(8,128)(2,1)} %parents.1, s32[1,256]{1,0:T(1,128)} %bitcast.9, s32[1,512]{1,0:T(1,128)} %bitcast.7, bf16[8,512]{1,0:T(8,128)(2,1)} %sib_in.1, f32[1,512]{1,0:T(1,128)} %bitcast.8, ...), custom_call_target="tpu_custom_call" | custom-call | tf_op jit(solution)/shard_map/train_step/pallas_call | solution.py:636
  91.1 4.7 %decode.1 = (f32[512,1536]{1,0:T(8,128)}, f32[512,512]{1,0:T(8,128)}, f32[8,512]{1,0:T(8,128)}, f32[1,512]{1,0:T(1,128)}, f32[8,512]{1,0:T(8,128)}) custom-call(s16[2,4,544,128]{3,2,1,0:T(8,128)(2,1)} %get-tuple-element.13.early_in, s16[2,4,544,128]{3,2,1,0:T(8,128)(2,1)} %get-tuple-element.14.late_in, f32[32,512]{1,0:T(8,128)} %get-tuple-element.15.small), custom_call_target="tpu_custom_call" | custom-call | tf_op jit(solution)/shard_map/decode/pallas_call | solution.py:652

commit v4 on v3

--- a/solution.py
+++ b/solution.py
@@ -572,8 +572,8 @@
     late[...] = dot_tn(normed[...], d_packed[:, pl.ds(D, 2 * D)])
     late_sum = reduce_all(at, links, late, l_r0, l_own, l_r1, l_z, l_r2, l_p, l_ag, l_pa, l_full)
     step(late_sum)
+    step(late_sum)
     step(early_sum)
-    step(late_sum)
     wide[...] += dot_nt(d_packed[:, pl.ds(D, 2 * D)], w_qkv[:, pl.ds(D, 2 * D)])
     grad_gain = jnp.zeros((1, D), F32)
     grad_sib = jnp.zeros((128, D), F32)
@@ -590,11 +590,10 @@
     small[pl.ds(16, 16), :] = grad_sib[16:32]
     small_sum = reduce_small(at, links, small, small_out, x0, x1, xz, xp)
     step(small_sum)
-    step(early_sum)
     more = True
     while more:
+        more = step(late_sum)
         step(small_sum)
-        more = step(late_sum)
         step(early_sum)
     finish(early_sum)
     finish(small_sum)

time: 96.2 us -> 90.6 us (0.942)
  Pallas kernels: 95.1 us -> 89.6 us
    pallas_call x1, Pallas kernels: 90.4 us -> 84.9 us  [shards(): pl.pallas_call(kernel, out_shape=[codes, codes, jax.ShapeDtypeStruct((32,...]
where the time goes in v4:
time: 90.6 us; the launch traced here: 90.4 us
  Pallas kernels  89.6 us (99%)
    pallas_call x1, Pallas kernels, shards(): pl.pallas_call(kernel, out_shape=[codes, codes, jax.ShapeDtypeStruct((32,...  84.9 us
    pallas_call x1, Pallas kernels, shards(): pl.pallas_call(decode, in_specs=[hbm, hbm, spec], out_specs=[hbm, hbm, sp...  4.73 us

profile of v4, /device:TPU:1, one launch (start us, length us, event | category | flops | bytes accessed | tf_op | source)
XLA Modules:
  0.0 90.4 jit_solution(9523962054412253188)
XLA Ops:
  0.6 84.9 %train_step.1 = (s16[2,4,544,128]{3,2,1,0:T(8,128)(2,1)}, s16[2,4,544,128]{3,2,1,0:T(8,128)(2,1)}, f32[32,512]{1,0:T(8,128)}) custom-call(bf16[256,512]{1,0:T(8,128)(2,1)} %parents.1, s32[1,256]{1,0:T(1,128)} %bitcast.9, s32[1,512]{1,0:T(1,128)} %bitcast.7, bf16[8,512]{1,0:T(8,128)(2,1)} %sib_in.1, f32[1,512]{1,0:T(1,128)} %bitcast.8, ...), custom_call_target="tpu_custom_call" | custom-call | tf_op jit(solution)/shard_map/train_step/pallas_call | solution.py:635
  85.5 4.7 %decode.1 = (f32[512,1536]{1,0:T(8,128)}, f32[512,512]{1,0:T(8,128)}, f32[8,512]{1,0:T(8,128)}, f32[1,512]{1,0:T(1,128)}, f32[8,512]{1,0:T(8,128)}) custom-call(s16[2,4,544,128]{3,2,1,0:T(8,128)(2,1)} %get-tuple-element.13.early_in, s16[2,4,544,128]{3,2,1,0:T(8,128)(2,1)} %get-tuple-element.14.late_in, f32[32,512]{1,0:T(8,128)} %get-tuple-element.15.small), custom_call_target="tpu_custom_call" | custom-call | tf_op jit(solution)/shard_map/decode/pallas_call | solution.py:651

commit v5 on v4

--- a/solution.py
+++ b/solution.py
@@ -409,14 +409,17 @@
     ends[1, 8:] = count[:8]
     count_col = count[:8].T[:, :1]
     start_col = (local_ends - count[:8]).T[:, :1]
-    for copy in loads[1:]:
+    for copy in loads[1:4]:
         copy.wait()
     for r in range(8):
         value = (window[own, :].astype(F32) + sib_table[r : r + 1, :].astype(F32)).astype(BF16).astype(F32)
         inverse = lax.rsqrt(jnp.mean(value * value, axis=-1, keepdims=True) + 1e-06)
         inverse = jnp.where(count_col > float(r), inverse, 0.0)
-        pair_rows[pl.ds(r * PAR, PAR), :] = (value * inverse * gain[...]).astype(BF16)
-    pair_kv[...] = dot(pair_rows[...], w_qkv[:, pl.ds(D, 2 * D)]).astype(BF16)
+        rows_r = (value * inverse * gain[...]).astype(BF16)
+        if r == 0:
+            for copy in loads[4:]:
+                copy.wait()
+        pair_kv[pl.ds(r * PAR, PAR), :] = dot(rows_r, w_qkv[:, pl.ds(D, 2 * D)]).astype(BF16)
     for h in range(HEADS):
         states[pl.ds(h * HS, HS), :] = dot_tn(pair_kv[:, head(h)], pair_kv[:, head(h, 1)])
     all_here()
@@ -470,8 +473,8 @@
         inverse = lax.rsqrt(jnp.mean(value * value, axis=-1, keepdims=True) + 1e-06)
         inv_in[block(b), :] = inverse
         normed[block(b), :] = (value * inverse * gain[...]).astype(BF16)
+    step(forward)
     packed[...] = dot(normed[...], w_qkv[...]).astype(BF16)
-    step(forward)
 
     for h in range(HEADS):
         for b in range(BLOCKS):

time: 90.6 us -> 89.4 us (0.987)
  Pallas kernels: 89.6 us -> 88.4 us
    pallas_call x1, Pallas kernels: 84.9 us -> 83.7 us  [shards(): pl.pallas_call(kernel, out_shape=[codes, codes, jax.ShapeDtypeStruct((32,...]
where the time goes in v5:
time: 89.4 us; the launch traced here: 89.2 us
  Pallas kernels  88.4 us (99%)
    pallas_call x1, Pallas kernels, shards(): pl.pallas_call(kernel, out_shape=[codes, codes, jax.ShapeDtypeStruct((32,...  83.7 us
    pallas_call x1, Pallas kernels, shards(): pl.pallas_call(decode, in_specs=[hbm, hbm, spec], out_specs=[hbm, hbm, sp...  4.73 us

profile of v5, /device:TPU:1, one launch (start us, length us, event | category | flops | bytes accessed | tf_op | source)
XLA Modules:
  0.0 89.2 jit_solution(7020260777719428308)
XLA Ops:
  0.6 83.7 %train_step.1 = (s16[2,4,544,128]{3,2,1,0:T(8,128)(2,1)}, s16[2,4,544,128]{3,2,1,0:T(8,128)(2,1)}, f32[32,512]{1,0:T(8,128)}) custom-call(bf16[256,512]{1,0:T(8,128)(2,1)} %parents.1, s32[1,256]{1,0:T(1,128)} %bitcast.9, s32[1,512]{1,0:T(1,128)} %bitcast.7, bf16[8,512]{1,0:T(8,128)(2,1)} %sib_in.1, f32[1,512]{1,0:T(1,128)} %bitcast.8, ...), custom_call_target="tpu_custom_call" | custom-call | tf_op jit(solution)/shard_map/train_step/pallas_call | solution.py:638
  84.3 4.7 %decode.1 = (f32[512,1536]{1,0:T(8,128)}, f32[512,512]{1,0:T(8,128)}, f32[8,512]{1,0:T(8,128)}, f32[1,512]{1,0:T(1,128)}, f32[8,512]{1,0:T(8,128)}) custom-call(s16[2,4,544,128]{3,2,1,0:T(8,128)(2,1)} %get-tuple-element.13.early_in, s16[2,4,544,128]{3,2,1,0:T(8,128)(2,1)} %get-tuple-element.14.late_in, f32[32,512]{1,0:T(8,128)} %get-tuple-element.15.small), custom_call_target="tpu_custom_call" | custom-call | tf_op jit(solution)/shard_map/decode/pallas_call | solution.py:654
